TPU v7x, 256 devices: a whole 4x4x8 slice. The times are simulated.
256 devices in a mesh: pts: 64 (over z, x, core), grp: 4 (over y).
Axes of the slice: x: 4, y: 4, z: 8, core: 2. Of those that a mesh axis runs over, the one named last changes fastest.
Arguments:
- feats: bfloat16 [262144, 256], P(('pts', 'grp')), may hold values from -8 to 8
- counts: int32 [256], P(('pts', 'grp')), may hold values from 512 to 1024, as said below
- parent: int32 [262144], P(('pts', 'grp')), may hold values from 0 to 65535, as said below
- ln_gain: float32 [256], replicated, may hold values from 0.5 to 1.5
- w_qkv: bfloat16 [256, 768], replicated, may hold values from -0.41015625 to 0.41015625
- w_out: bfloat16 [256, 256], replicated, may hold values from -0.375 to 0.375
- w_down: bfloat16 [256, 512], replicated, may hold values from -0.375 to 0.375
- w_up: bfloat16 [512, 256], replicated, may hold values from -0.25 to 0.25
- cotangent: bfloat16 [262144, 256], P(('pts', 'grp')), may hold values from -6 to 6
Outputs:
- result: bfloat16 [262144, 256], P(('pts', 'grp'))
- d_feats: bfloat16 [262144, 256], P(('pts', 'grp'))
- grad_qkv: float32 [256, 768], replicated
- grad_out: float32 [256, 256], replicated
- grad_down: float32 [256, 512], replicated
- grad_up: float32 [512, 256], replicated
Inputs may be any that keep to these rules, and one draw needn't show every extreme that they name: `counts`: the device holding the most live points holds 1024 of them; every device holds at least 512. `parent`: within each device's 1024 rows parents never fall. A live row of device d names a coarse row from d * 256 to d * 256 + 320 - 1 (the last device: its own 256 rows only), and its last live row names the last of these.
All inputs are finite; a program needn't handle non-finite values.
Results may differ from a plain program's by a relative error of at most 0.012.
The roundings to bfloat16 on the way count: a program that leaves them out, or rounds other values in their place, can miss the bound.
Values may be sent and summed in bfloat16 or wider, within the bound.
A program may use at most 64 MiB of HBM per device.

v0:
```python
import jax
import jax.numpy as jnp
from jax import lax
from jax.sharding import PartitionSpec as P

HD = 16
PATCH = 1024
RATIO = 4
SPILL = 64
HGROUP = 2


def shifted(block, axis, distance):
    devices = range(lax.axis_size(axis))
    route = [(i - distance, i) for i in devices if i - distance in devices]
    return lax.ppermute(block, axis, route)


def layer_norm(values, ln_gain):
    center = values - jnp.mean(values, axis=-1, keepdims=True)
    spread = jnp.mean(center * center, axis=-1, keepdims=True)
    return center * lax.rsqrt(spread + 1e-05) * ln_gain


def attend(query, keys, values, key_live):
    scores = jnp.einsum("grd,gsd->grs", query, keys, preferred_element_type=jnp.float32) * HD ** (
        -0.5
    )
    scores = jnp.where(key_live[None, None, :], scores, -1e30)
    highest = jnp.max(scores, axis=-1, keepdims=True)
    raised = jnp.exp(scores - highest)
    probs = (raised / jnp.sum(raised, axis=-1, keepdims=True)).astype(jnp.bfloat16)
    mixed = jnp.einsum("grs,gsd->grd", probs, values, preferred_element_type=jnp.float32)
    return mixed.astype(jnp.bfloat16)


def heads_first(block, width):
    return block.reshape(block.shape[0], width // (HGROUP * HD), HGROUP, HD).transpose(1, 2, 0, 3)


def heads_last(block):
    return block.transpose(2, 0, 1, 3).reshape(block.shape[2], -1)


def split_parts(proj_rows):
    width = proj_rows.shape[1] // 3
    query = heads_first(proj_rows[:, :width], width)
    keys = heads_first(proj_rows[:, width : 2 * width], width)
    values = heads_first(proj_rows[:, 2 * width :], width)
    return (query, keys, values, width)


def patch_forward(proj_rows, key_live):
    query, keys, values, width = split_parts(proj_rows)

    def one_group(group):
        return attend(group[0], group[1], group[2], key_live)

    return heads_last(lax.map(one_group, (query, keys, values)))


def patch_backward(proj_rows, key_live, d_attended):
    query, keys, values, width = split_parts(proj_rows)
    d_heads = heads_first(d_attended, width)

    def one_group(group):

        def inner(query_g, keys_g, values_g):
            return attend(query_g, keys_g, values_g, key_live)

        _, pull = jax.vjp(inner, group[0], group[1], group[2])
        return pull(group[3])

    d_query, d_keys, d_values = lax.map(one_group, (query, keys, values, d_heads))
    return jnp.concatenate([heads_last(d_query), heads_last(d_keys), heads_last(d_values)], axis=1)


def inner_rows(left, right):
    return lax.dot_general(
        left, right, (((0,), (0,)), ((), ())), preferred_element_type=jnp.float32
    )


def times_transposed(left, right):
    return lax.dot_general(
        left, right, (((1,), (1,)), ((), ())), preferred_element_type=jnp.float32
    )


def add_front(block, extra):
    return jnp.concatenate([block[: extra.shape[0]] + extra, block[extra.shape[0] :]], axis=0)


def per_device(feats, counts, parent, ln_gain, w_qkv, w_out, w_down, w_up, cotangent):
    rows_here = feats.shape[0]
    width = feats.shape[1]
    core_rows = rows_here // RATIO
    table_rows = core_rows + SPILL
    device_index = lax.axis_index(("pts", "grp"))
    live_rows = jnp.arange(rows_here, dtype=jnp.int32) < counts[0]
    local_parent = parent - device_index * core_rows
    member = (
        local_parent[None, :] == jnp.arange(table_rows, dtype=jnp.int32)[:, None]
    ) & live_rows[None, :]
    member_b = member.astype(jnp.bfloat16)
    feats_wide = feats.astype(jnp.float32)
    normed = layer_norm(feats_wide, ln_gain).astype(jnp.bfloat16)
    proj = jnp.dot(normed, w_qkv, preferred_element_type=jnp.float32).astype(jnp.bfloat16)
    proj_patches = proj.reshape(rows_here // PATCH, PATCH, 3 * width)
    key_live = live_rows.reshape(rows_here // PATCH, PATCH)

    def forward_one(pair):
        return patch_forward(pair[0], pair[1])

    attended = lax.map(forward_one, (proj_patches, key_live)).reshape(rows_here, width)
    hidden = (feats_wide + jnp.dot(attended, w_out, preferred_element_type=jnp.float32)).astype(
        jnp.bfloat16
    )
    pooled_sum = jnp.dot(member_b, hidden, preferred_element_type=jnp.float32)
    child_count = jnp.sum(member.astype(jnp.float32), axis=1)
    sum_in, count_in = (
        shifted(pooled_sum[core_rows:].astype(jnp.bfloat16), ("pts", "grp"), 1).astype(jnp.float32),
        shifted(child_count[core_rows:].astype(jnp.bfloat16), ("pts", "grp"), 1).astype(
            jnp.float32
        ),
    )
    own_sum = add_front(pooled_sum[:core_rows], sum_in)
    denominator = jnp.maximum(add_front(child_count[:core_rows], count_in), 1.0)
    pooled = (own_sum / denominator[:, None]).astype(jnp.bfloat16)
    pre = jnp.dot(pooled, w_down, preferred_element_type=jnp.float32)
    activ = jax.nn.gelu(pre).astype(jnp.bfloat16)
    back = jnp.dot(activ, w_up, preferred_element_type=jnp.float32).astype(jnp.bfloat16)
    back_next = shifted(back[:SPILL], ("pts", "grp"), -1)
    safe_parent = jnp.clip(local_parent, 0, table_rows - 1)
    back_table = jnp.concatenate([back, back_next], axis=0)
    unpooled = jnp.where(
        live_rows[:, None], jnp.take(back_table, safe_parent, axis=0).astype(jnp.float32), 0.0
    )
    result = (hidden.astype(jnp.float32) + unpooled).astype(jnp.bfloat16)
    cot_sum = jnp.dot(member_b, cotangent, preferred_element_type=jnp.float32)
    cot_in = shifted(cot_sum[core_rows:].astype(jnp.bfloat16), ("pts", "grp"), 1).astype(
        jnp.float32
    )
    d_back = add_front(cot_sum[:core_rows], cot_in).astype(jnp.bfloat16)
    d_gelu = times_transposed(d_back, w_up)
    _, gelu_pull = jax.vjp(jax.nn.gelu, pre)
    d_pre = gelu_pull(d_gelu)[0].astype(jnp.bfloat16)
    grad_up_part = inner_rows(activ, d_back)
    grad_down_part = inner_rows(pooled, d_pre)
    d_share = times_transposed(d_pre, w_down) / denominator[:, None]
    share_next = shifted(d_share[:SPILL].astype(jnp.bfloat16), ("pts", "grp"), -1).astype(
        jnp.float32
    )
    share_table = jnp.concatenate([d_share, share_next], axis=0)
    d_hidden = cotangent.astype(jnp.float32) + jnp.where(
        live_rows[:, None], jnp.take(share_table, safe_parent, axis=0), 0.0
    )
    d_hidden_b = d_hidden.astype(jnp.bfloat16)
    grad_out_part = inner_rows(attended, d_hidden_b)
    d_attended = times_transposed(d_hidden_b, w_out).astype(jnp.bfloat16)

    def backward_one(triple):
        return patch_backward(triple[0], triple[1], triple[2])

    d_proj = lax.map(
        backward_one, (proj_patches, key_live, d_attended.reshape(rows_here // PATCH, PATCH, width))
    ).reshape(rows_here, 3 * width)
    grad_qkv_part = inner_rows(normed, d_proj)
    d_normed = times_transposed(d_proj, w_qkv)

    def norm_only(values):
        return layer_norm(values, ln_gain)

    _, norm_pull = jax.vjp(norm_only, feats_wide)
    d_feats = (d_hidden + norm_pull(d_normed)[0]).astype(jnp.bfloat16)
    grad_qkv, grad_out, grad_down, grad_up = lax.psum(
        (grad_qkv_part, grad_out_part, grad_down_part, grad_up_part), ("pts", "grp")
    )
    return (result, d_feats, grad_qkv, grad_out, grad_down, grad_up)


def solution(mesh):
    in_specs = (
        P(("pts", "grp"), None),
        P(("pts", "grp")),
        P(("pts", "grp")),
        P(),
        P(),
        P(),
        P(),
        P(),
        P(("pts", "grp"), None),
    )
    out_specs = (P(("pts", "grp"), None), P(("pts", "grp"), None), P(), P(), P(), P())
    return jax.shard_map(
        per_device, mesh=mesh, in_specs=in_specs, out_specs=out_specs, check_vma=False
    )
```

profile of v0, /device:TPU:1, one launch (start us, length us, event | category | flops | bytes accessed | tf_op | source)
XLA Modules:
  0.0 619.2 jit_solution(18052785459150442315)
XLA Ops:
  10.0 4.0 collective-permute-start.1
  16.2 3.2 collective-permute-start.3
  25.5 87.0 %while.42 = (s32[]{:T(128)}, bf16[8,2,1024,16]{2,3,1,0:T(8,128)(2,1)S(1)}, bf16[8,2,1024,16]{2,3,1,0:T(8,128)(2,1)S(1)}, bf16[8,2,1024,16]{2,3,1,0:T(8,128)(2,1)...) while((s32[]{:T(128)}, bf16[8,2,1024,16]{2,3,1,0:T(8,128)(2,1)S(1)}, ...), condition=%wide.region_5.6_spmd.clone, body=%wide.region_2.5_spmd.clone.sunk | while | flops 146835456 | bytes 17059928 | solution.py:59
  26.2 6.2 fusion.186
  32.4 4.0 fusion.187
  37.1 6.2 fusion.186
  43.2 4.0 fusion.187
  47.9 6.2 fusion.186
  54.1 4.0 fusion.187
  58.8 6.2 fusion.186
  65.0 4.0 fusion.187
  69.7 6.2 fusion.186
  75.8 4.0 fusion.187
  80.5 6.2 fusion.186
  86.7 4.0 fusion.187
  91.4 6.2 fusion.186
  97.6 4.0 fusion.187
  102.3 6.2 fusion.186
  108.4 4.0 fusion.187
  113.3 2.9 collective-permute-start
  126.2 2.9 collective-permute-start.4
  130.9 3.3 collective-permute-start.2
  134.3 3.5 gather_fusion.1
  140.3 192.1 %while.43 = (s32[]{:T(128)}, bf16[8,2,1024,16]{2,3,1,0:T(8,128)(2,1)}, bf16[8,2,1024,16]{2,3,1,0:T(8,128)(2,1)S(1)}, bf16[8,2,1024,16]{2,3,1,0:T(8,128)(2,1)S(1)...) while((s32[]{:T(128)}, ...), condition=%wide.region_13.14_spmd.clone, body=%wide.region_7.13_spmd.clone.sunk | while | flops 417432576 | bytes 82637936 | solution.py:74
  146.0 3.0 fusion.196
  149.0 5.7 convert_reduce_fusion.4
  154.8 3.5 fusion.193
  158.4 3.6 fusion.195
  161.9 2.6 fusion.194
  170.0 3.0 fusion.196
  173.0 5.7 convert_reduce_fusion.4
  178.8 3.5 fusion.193
  182.3 3.6 fusion.195
  185.9 2.6 fusion.194
  194.0 3.0 fusion.196
  197.0 5.7 convert_reduce_fusion.4
  202.8 3.5 fusion.193
  206.3 3.6 fusion.195
  209.9 2.6 fusion.194
  218.0 3.0 fusion.196
  221.0 5.8 convert_reduce_fusion.4
  226.8 3.5 fusion.193
  230.3 3.6 fusion.195
  242.0 3.0 fusion.196
  245.0 5.7 convert_reduce_fusion.4
  250.8 3.5 fusion.193
  254.3 3.6 fusion.195
  266.0 3.0 fusion.196
  269.0 5.7 convert_reduce_fusion.4
  274.8 3.5 fusion.193
  278.3 3.6 fusion.195
  290.0 3.0 fusion.196
  293.0 5.8 convert_reduce_fusion.4
  298.8 3.5 fusion.193
  302.3 3.6 fusion.195
  314.0 3.0 fusion.196
  317.0 5.7 convert_reduce_fusion.4
  322.8 3.5 fusion.193
  326.3 3.6 fusion.195
  333.5 2.9 fusion.112
  336.3 2.8 fusion.107
  341.2 5.0 gather_fusion
  347.5 4.1 add_convert_fusion
  351.6 253.3 %all-reduce.3.cloned.1.call-done = (f32[256,768]{1,0:T(8,128)}, f32[256,256]{1,0:T(8,128)}, f32[256,512]{1,0:T(8,128)}, f32[512,256]{1,0:T(8,128)}) async-done(((f32[256,768]{1,0:T(8,128)}, f32[256,256]{1,0:T(8,128)}, f32[256,512]{1,0:T(8,128)}, f32[512,256]{1,0:T(8,128)}), (f32[256,768]{1,0:T(8,128)}, f32[256,256]{1,0:T(8,128)}, f32[256,512]{1,0:T(8,128)}, ...) | async-done | bytes 2097168 | tf_op jit(solution)/shard_map/psum | solution.py:176
  (176 shorter events, 98.9 us)
Async XLA Ops:
  7.2 16.1 %copy-start = (bf16[256,768]{1,0:T(8,128)(2,1)S(1)}, bf16[256,768]{1,0:T(8,128)(2,1)}, u32[]{:S(2)}) copy-start(bf16[256,768]{1,0:T(8,128)(2,1)} %param.17) | copy-start | bytes 1179652
  7.2 597.7 %all-reduce.3.cloned.1.call-start = ((), (), s32[]{:S(2)}) async-start(), calls=%async_computation | async-start | bytes 4194304 | tf_op jit(solution)/shard_map/psum | solution.py:176
  9.2 128.6 %copy-start.26 = (pred[1024]{0:T(1024)(128)(4,1)}, pred[1024]{0:T(1024)(128)(4,1)S(1)}, u32[]{:S(2)}) copy-start(pred[1024]{0:T(1024)(128)(4,1)S(1)} %get-tuple-element.209) | copy-start | bytes 3076
  10.0 107.2 %collective-permute-start.1 = (bf16[64]{0:T(256)(128)(2,1)}, bf16[64]{0:T(256)(128)(2,1)}, u32[]{:S(2)}, u32[]{:S(2)}) collective-permute-start(bf16[64]{0:T(256)(128)(2,1)} %slice.72), channel_id=1, source_target_pairs={{0,1},{1,2},{2,3},{3,4},{4,5},{5,6},{6,7},{7,8},{8,9},{9,10},{10,1... | collective-permute-start | bytes 392 | tf_op jit(solution)/shard_map/ppermute | solution.py:16
  16.2 5.9 copy-start.17
  16.2 106.0 %collective-permute-start.3 = (bf16[64,256]{1,0:T(8,128)(2,1)S(1)}, bf16[64,256]{1,0:T(8,128)(2,1)S(1)}, u32[]{:S(2)}, u32[]{:S(2)}) collective-permute-start(bf16[64,256]{1,0:T(8,128)(2,1)S(1)} %slice.91), channel_id=1, source_target_pairs={{0,1},{1,2},{2,3},{3,4},{4,5},{5,6},{6,7},{7,8},{8,9},{9,10},{10,1... | collective-permute-start | bytes 98312 | tf_op jit(solution)/shard_map/ppermute | solution.py:16
  20.7 1.5 copy-start.18
  22.1 0.6 copy-start.22
  22.7 0.6 copy-start.20
  25.5 87.1 %copy-start.1 = (bf16[1024,256]{1,0:T(8,128)(2,1)S(1)}, bf16[1024,256]{1,0:T(8,128)(2,1)}, u32[]{:S(2)}) copy-start(bf16[1024,256]{1,0:T(8,128)(2,1)} %param.13) | copy-start | bytes 1572868
  25.5 87.1 %copy-start.15 = (bf16[256,256]{1,0:T(8,128)(2,1)S(1)}, bf16[256,256]{1,0:T(8,128)(2,1)}, u32[]{:S(2)}) copy-start(bf16[256,256]{1,0:T(8,128)(2,1)} %param.18) | copy-start | bytes 393220
  112.5 21.8 %copy-start.7 = (bf16[8,2,1024,16]{2,3,1,0:T(8,128)(2,1)}, bf16[8,2,1024,16]{2,3,1,0:T(8,128)(2,1)S(1)}, u32[]{:S(2)}) copy-start(bf16[8,2,1024,16]{2,3,1,0:T(8,128)(2,1)S(1)} %get-tuple-element.114) | copy-start | bytes 1572868
  112.5 21.8 %copy-start.11 = (bf16[8,2,1024,16]{2,3,1,0:T(8,128)(2,1)}, bf16[8,2,1024,16]{2,3,1,0:T(8,128)(2,1)S(1)}, u32[]{:S(2)}) copy-start(bf16[8,2,1024,16]{2,3,1,0:T(8,128)(2,1)S(1)} %get-tuple-element.388) | copy-start | bytes 1572868
  112.5 21.8 %copy-start.14 = (bf16[8,2,1024,16]{2,3,1,0:T(8,128)(2,1)}, bf16[8,2,1024,16]{2,3,1,0:T(8,128)(2,1)S(1)}, u32[]{:S(2)}) copy-start(bf16[8,2,1024,16]{2,3,1,0:T(8,128)(2,1)S(1)} %get-tuple-element.396) | copy-start | bytes 1572868
  112.5 13.4 %copy-start.29 = (bf16[256,512]{1,0:T(8,128)(2,1)S(1)}, bf16[256,512]{1,0:T(8,128)(2,1)}, u32[]{:S(2)}) copy-start(bf16[256,512]{1,0:T(8,128)(2,1)} %param.19) | copy-start | bytes 786436
  112.9 21.4 %copy-start.10 = (bf16[1024,256]{1,0:T(8,128)(2,1)}, bf16[1024,256]{1,0:T(8,128)(2,1)S(1)}, u32[]{:S(2)}) copy-start(bf16[1024,256]{1,0:T(8,128)(2,1)S(1)} %fusion.103) | copy-start | bytes 1572868
  113.3 6.4 %collective-permute-start = (bf16[64,256]{1,0:T(8,128)(2,1)S(1)}, bf16[64,256]{1,0:T(8,128)(2,1)S(1)}, u32[]{:S(2)}, u32[]{:S(2)}) collective-permute-start(bf16[64,256]{1,0:T(8,128)(2,1)S(1)} %slice.102), channel_id=1, source_target_pairs={{0,1},{1,2},{2,3},{3,4},{4,5},{5,6},{6,7},{7,8},{8,9},{9,10},{10,1... | collective-permute-start | bytes 98312 | tf_op jit(solution)/shard_map/ppermute | solution.py:16
  116.3 21.5 %copy-start.24 = (s32[1024]{0:T(1024)}, s32[1024]{0:T(1024)S(1)}, u32[]{:S(2)}) copy-start(s32[1024]{0:T(1024)S(1)} %fusion.126) | copy-start | bytes 12292
  122.2 12.0 %copy-start.16 = (bf16[256,256]{1,0:T(8,128)(2,1)}, bf16[256,256]{1,0:T(8,128)(2,1)S(1)}, u32[]{:S(2)}) copy-start(bf16[256,256]{1,0:T(8,128)(2,1)S(1)} %convolution_convert_fusion.3) | copy-start | bytes 393220
  123.2 14.6 %copy-start.9 = (bf16[1024,256]{1,0:T(8,128)(2,1)S(1)}, bf16[1024,256]{1,0:T(8,128)(2,1)}, u32[]{:S(2)}) copy-start(bf16[1024,256]{1,0:T(8,128)(2,1)} %param.21) | copy-start | bytes 1572868
  123.2 14.6 %copy-start.27 = (pred[1024]{0:T(1024)(128)(4,1)S(1)}, pred[1024]{0:T(1024)(128)(4,1)}, u32[]{:S(2)}) copy-start(pred[1024]{0:T(1024)(128)(4,1)} %get-tuple-element.192) | copy-start | bytes 3076
  126.2 8.0 %collective-permute-start.4 = (bf16[64,256]{1,0:T(8,128)(2,1)S(1)}, bf16[64,256]{1,0:T(8,128)(2,1)S(1)}, u32[]{:S(2)}, u32[]{:S(2)}) collective-permute-start(bf16[64,256]{1,0:T(8,128)(2,1)S(1)} %slice.101), channel_id=1, source_target_pairs={{1,0},{2,1},{3,2},{4,3},{5,4},{6,5},{7,6},{8,7},{9,8},{10,9},{11,1... | collective-permute-start | bytes 98312 | tf_op jit(solution)/shard_map/ppermute | solution.py:16
  130.9 209.3 %collective-permute-start.2 = (bf16[64,256]{1,0:T(8,128)(2,1)}, bf16[64,256]{1,0:T(8,128)(2,1)}, u32[]{:S(2)}, u32[]{:S(2)}) collective-permute-start(bf16[64,256]{1,0:T(8,128)(2,1)} %slice.89), channel_id=1, source_target_pairs={{1,0},{2,1},{3,2},{4,3},{5,4},{6,5},{7,6},{8,7},{9,8},{10,9},{11,1... | collective-permute-start | bytes 98312 | tf_op jit(solution)/shard_map/ppermute | solution.py:16
  137.8 2.5 copy-start.3
  138.2 2.1 copy-start.5
  140.3 193.1 %copy-start.2 = (bf16[1024,256]{1,0:T(8,128)(2,1)S(1)}, bf16[1024,256]{1,0:T(8,128)(2,1)}, u32[]{:S(2)}) copy-start(bf16[1024,256]{1,0:T(8,128)(2,1)} %param.13) | copy-start | bytes 1572868
  140.3 193.1 %copy-start.19 = (f32[1024]{0:T(1024)S(1)}, f32[1024]{0:T(1024)}, u32[]{:S(2)}) copy-start(f32[1024]{0:T(1024)} %copy-done.18) | copy-start | bytes 12292
  140.3 193.1 %copy-start.21 = (f32[1024]{0:T(1024)S(1)}, f32[1024]{0:T(1024)}, u32[]{:S(2)}) copy-start(f32[1024]{0:T(1024)} %copy-done.20) | copy-start | bytes 12292
  140.3 193.1 %copy-start.28 = (f32[256]{0:T(256)S(1)}, f32[256]{0:T(256)}, u32[]{:S(2)}) copy-start(f32[256]{0:T(256)} %param.16) | copy-start | bytes 3076
  332.5 0.8 copy-start.12
  332.5 1.0 copy-start.13
  332.5 6.7 %copy-start.6 = (bf16[1024,256]{1,0:T(8,128)(2,1)S(1)}, bf16[1024,256]{1,0:T(8,128)(2,1)}, u32[]{:S(2)}) copy-start(bf16[1024,256]{1,0:T(8,128)(2,1)} %copy-done.5) | copy-start | bytes 1572868
  332.5 6.7 %copy-start.8 = (bf16[8,2,1024,16]{2,3,1,0:T(8,128)(2,1)S(1)}, bf16[8,2,1024,16]{2,3,1,0:T(8,128)(2,1)}, u32[]{:S(2)}) copy-start(bf16[8,2,1024,16]{2,3,1,0:T(8,128)(2,1)} %copy-done.7) | copy-start | bytes 1572868
  332.5 8.7 %copy-start.25 = (s32[1024]{0:T(1024)S(1)}, s32[1024]{0:T(1024)}, u32[]{:S(2)}) copy-start(s32[1024]{0:T(1024)} %copy-done.24) | copy-start | bytes 12292
  336.3 9.8 %copy-start.23 = (f32[1024]{0:T(1024)S(1)}, f32[1024]{0:T(1024)}, u32[]{:S(2)}) copy-start(f32[1024]{0:T(1024)} %copy-done.22) | copy-start | bytes 12292
  336.3 11.2 %copy-start.4 = (f32[1024,256]{1,0:T(8,128)S(1)}, f32[1024,256]{1,0:T(8,128)}, u32[]{:S(2)}) copy-start(f32[1024,256]{1,0:T(8,128)} %copy-done.3) | copy-start | bytes 3145732
Sparse Core Ops, SparseCore 0:
  340.3 264.4 all-reduce.2
where the time goes:
time: 623 us; the launch traced here: 619 us
  waiting for transfers between devices  255 us (41%)
  matrix products  240 us (39%)
  other arithmetic  70.1 us (11%)
  local copies, waits for them, and re-layouts  21.4 us (3%)
  starting transfers between devices  16.4 us (3%)
  between operations  15.3 us (2%)
    psum x1, waiting for transfers between devices, per_device(): lax.psum((grad_qkv_part, grad_out_part, grad_down_part, grad_up_part), ('...  253 us
    dot_general x24, matrix products, attend(): jnp.einsum('grs,gsd->grd', probs, values, preferred_element_type=jnp.floa...  103 us
    dot_general x24, matrix products, attend(): jnp.einsum('grd,gsd->grs', query, keys, preferred_element_type=jnp.float32)  68.9 us
    sub x8, matrix products, attend(): raised = jnp.exp(scores - highest)  49.3 us
    reduce_sum x8, other arithmetic, attend(): raised = jnp.exp(scores - highest)  28.1 us
    reduce_sum x8, other arithmetic, attend(): jnp.sum(raised, axis=-1, keepdims=True)  18.7 us
    ppermute x5, starting transfers between devices, shifted(): return lax.ppermute(block, axis, route)  16.4 us
  transfers between devices with their start and end apart: 6, of which 2 were waited for; matrix products, arithmetic and copies ran while one was open for 51% of the time, Pallas kernels for 0%

commit v1 on v0

v1 whole, which is shorter than its diff:
```python
import functools

import jax
import jax.numpy as jnp
from jax import lax
from jax.experimental import pallas as pl
from jax.experimental.pallas import tpu as pltpu
from jax.sharding import PartitionSpec as P

HD = 16
HEADS = 16
ROWS = 1024
C1 = 256
C2 = 512
CORE = 256
SPILL = 64
TABLE = CORE + SPILL
PAIR = 2
STEPS = HEADS // PAIR
HALF = 128
SAFE_SCORE = 60.0
MESH = pl.DeviceIdType.MESH
BF = jnp.bfloat16
F32 = jnp.float32


def dg(left, right, left_dim, right_dim):
    return lax.dot_general(
        left,
        right,
        (((left_dim,), (right_dim,)), ((), ())),
        preferred_element_type=F32,
    )


def iota(shape, dim):
    return lax.broadcasted_iota(jnp.int32, shape, dim)


def norm_parts(wide):
    center = wide - jnp.mean(wide, axis=-1, keepdims=True)
    spread = jnp.mean(center * center, axis=-1, keepdims=True)
    inverse = lax.rsqrt(spread + 1e-05)
    return center * inverse, inverse


def device_number():
    return lax.axis_index("pts") * lax.axis_size("grp") + lax.axis_index("grp")


def whole(shape):
    return pl.BlockSpec(shape, lambda i, n=len(shape): (0,) * n)


def per_pair(rows):
    return pl.BlockSpec((PAIR, rows, ROWS), lambda i: (i, 0, 0))


def forward_kernel(
    counts_ref, parent_ref, feats_ref, gain_ref, w_qkv_ref, w_out_ref, cot_ref,
    raised_ref, proj_ref, scale_ref, att_ref, hidden_ref, sum_ref, count_ref, cot_sum_ref,
    keys_s, query_s, values_s, mixed_s, safe_s,
):
    step = pl.program_id(0)
    live = counts_ref[0]

    @pl.when(step == 0)
    def _():
        xhat, _ = norm_parts(feats_ref[...].astype(F32))
        normed = (xhat * gain_ref[...]).astype(BF)
        proj = dg(w_qkv_ref[...], normed, 0, 1).astype(BF)
        proj_ref[...] = proj
        keys = dg(normed, w_qkv_ref[:, C1 : 2 * C1], 1, 0).astype(BF)
        dead = (iota((ROWS, HALF), 0) >= live) & (iota((ROWS, HALF), 1) == 0)
        bias = jnp.where(dead, -1e30, 0.0).astype(BF)
        for half in range(2):
            keys_s[half, :, :HALF] = keys[:, half * HALF : (half + 1) * HALF]
            keys_s[half, :, HALF:] = bias
        ones = jnp.where(iota((HALF, ROWS), 0) == 0, 1.0, 0.0).astype(BF)
        for one in range(PAIR):
            query_s[one, HALF:, :] = ones
            values_s[one, HD:, :] = jnp.ones((HD, ROWS), BF)
        wide = proj[: 2 * C1, :].astype(F32)
        squares = jnp.sum((wide * wide).reshape(2, HEADS, HD, ROWS), axis=2)
        bound = jnp.max(squares[0]) * jnp.max(squares[1]) / HD
        safe_s[0] = (bound <= SAFE_SCORE * SAFE_SCORE).astype(jnp.int32)

    half = step // (STEPS // 2)
    for one in range(PAIR):
        head = step * PAIR + one
        start = pl.multiple_of(head * HD, HD)
        place = pl.multiple_of(lax.rem(head, HEADS // 2) * HD, HD)
        query_s[one, :HALF, :] = jnp.zeros((HALF, ROWS), BF)
        query_s[one, pl.ds(place, HD), :] = proj_ref[pl.ds(start, HD), :] * jnp.asarray(
            HD ** (-0.5), BF
        )
        values_s[one, :HD, :] = proj_ref[pl.ds(2 * C1 + start, HD), :]

    @pl.when(safe_s[0] == 1)
    def _():
        for one in range(PAIR):
            raised = jnp.exp(dg(keys_s[half], query_s[one], 1, 0)).astype(BF)
            raised_ref[one] = raised
            mixed_s[one] = dg(values_s[one], raised, 1, 0)

    @pl.when(safe_s[0] != 1)
    def _():
        for one in range(PAIR):
            scores = dg(keys_s[half], query_s[one], 1, 0)
            highest = jnp.max(scores, axis=0, keepdims=True)
            raised = jnp.exp(scores - highest).astype(BF)
            raised_ref[one] = raised
            mixed_s[one] = dg(values_s[one], raised, 1, 0)

    for one in range(PAIR):
        start = pl.multiple_of((step * PAIR + one) * HD, HD)
        scale = 1.0 / mixed_s[one, HD:, :]
        att_ref[pl.ds(start, HD), :] = (mixed_s[one, :HD, :] * scale).astype(BF)
        scale_ref[one] = scale[:8]

    @pl.when(step == STEPS - 1)
    def _():
        attended = att_ref[...].T
        hidden = (
            feats_ref[...].astype(F32) + dg(attended, w_out_ref[...], 1, 0)
        ).astype(BF)
        hidden_ref[...] = hidden
        local = parent_ref[...] - device_number() * CORE
        member = (local == iota((TABLE, ROWS), 0)) & (iota((TABLE, ROWS), 1) < live)
        member_f = jnp.where(member, 1.0, 0.0)
        count_ref[...] = jnp.broadcast_to(
            jnp.sum(member_f, axis=1, keepdims=True), (TABLE, HALF)
        )
        member_b = member_f.astype(BF)
        sum_ref[...] = dg(member_b, hidden, 1, 0)
        cot_sum_ref[...] = dg(member_b, cot_ref[...], 1, 0)


def forward_call(counts, parent, feats, gain, w_qkv, w_out, cotangent):
    out = jax.ShapeDtypeStruct
    return pl.pallas_call(
        forward_kernel,
        grid=(STEPS,),
        in_specs=[
            pl.BlockSpec(memory_space=pltpu.SMEM),
            whole((1, ROWS)),
            whole((ROWS, C1)),
            whole((1, C1)),
            whole((C1, 3 * C1)),
            whole((C1, C1)),
            whole((ROWS, C1)),
        ],
        out_specs=[
            per_pair(ROWS),
            whole((3 * C1, ROWS)),
            per_pair(8),
            whole((C1, ROWS)),
            whole((ROWS, C1)),
            whole((TABLE, C1)),
            whole((TABLE, HALF)),
            whole((TABLE, C1)),
        ],
        out_shape=[
            out((HEADS, ROWS, ROWS), BF),
            out((3 * C1, ROWS), BF),
            out((HEADS, 8, ROWS), F32),
            out((C1, ROWS), BF),
            out((ROWS, C1), BF),
            out((TABLE, C1), F32),
            out((TABLE, HALF), F32),
            out((TABLE, C1), F32),
        ],
        scratch_shapes=[
            pltpu.VMEM((2, ROWS, C1), BF),
            pltpu.VMEM((PAIR, C1, ROWS), BF),
            pltpu.VMEM((PAIR, 2 * HD, ROWS), BF),
            pltpu.VMEM((PAIR, 2 * HD, ROWS), F32),
            pltpu.SMEM((1,), jnp.int32),
        ],
        compiler_params=pltpu.CompilerParams(vmem_limit_bytes=56 * 2**20),
        name="forward",
    )(counts, parent, feats, gain, w_qkv, w_out, cotangent)


def gelu_and_slope(pre):
    root = 0.7978845608028654
    square = pre * pre
    tanh = jnp.tanh(root * (pre + 0.044715 * (square * pre)))
    value = pre * (0.5 * (1.0 + tanh))
    slope = 0.5 * (1.0 + tanh) + 0.5 * pre * (1.0 - tanh * tanh) * root * (
        1.0 + 3 * 0.044715 * square
    )
    return value, slope


def neighbour(distance):
    devices = lax.axis_size("pts") * lax.axis_size("grp")
    other = lax.rem(device_number() + distance + devices, devices)
    return (other // lax.axis_size("grp"), lax.rem(other, lax.axis_size("grp")))


def coarse_kernel(
    sum_ref, count_ref, cot_sum_ref, w_down_ref, w_up_ref,
    back_ref, share_ref, low_ref, grad_up_ref, grad_down_ref,
    send_up, recv_up, send_down, recv_down, send_sem, recv_sem,
):
    after, before = neighbour(1), neighbour(-1)
    barrier = pltpu.get_barrier_semaphore()
    for other in (after, before):
        pl.semaphore_signal(barrier, inc=1, device_id=other, device_id_type=MESH)
    send_up[:, :C1] = sum_ref[CORE:, :].astype(BF)
    send_up[:, C1 : 2 * C1] = cot_sum_ref[CORE:, :].astype(BF)
    spilled = count_ref[CORE:, :]
    high = spilled.astype(BF)
    low = (spilled - high.astype(F32)).astype(BF)
    send_up[:, 2 * C1 :] = jnp.where(iota((SPILL, HALF), 1) < HALF // 2, high, low)
    pl.semaphore_wait(barrier, 2)
    up = pltpu.make_async_remote_copy(
        send_up, recv_up, send_sem.at[0], recv_sem.at[0],
        device_id=after, device_id_type=MESH,
    )
    up.start()
    up.wait()
    got = recv_up[...].astype(F32)
    count_in = got[:, 2 * C1 : 2 * C1 + 1] + got[:, 2 * C1 + HALF // 2 : 2 * C1 + HALF // 2 + 1]
    own_sum = jnp.concatenate([sum_ref[:SPILL, :] + got[:, :C1], sum_ref[SPILL:CORE, :]], axis=0)
    own_cot = jnp.concatenate(
        [cot_sum_ref[:SPILL, :] + got[:, C1 : 2 * C1], cot_sum_ref[SPILL:CORE, :]], axis=0
    )
    counted = jnp.concatenate(
        [count_ref[:SPILL, :1] + count_in, count_ref[SPILL:CORE, :1]], axis=0
    )
    inverse = 1.0 / jnp.maximum(counted, 1.0)
    pooled = (own_sum * inverse).astype(BF)
    pre = dg(pooled, w_down_ref[...], 1, 0)
    value, slope = gelu_and_slope(pre)
    activ = value.astype(BF)
    back = dg(activ, w_up_ref[...], 1, 0).astype(BF)
    d_back = own_cot.astype(BF)
    d_pre = (dg(d_back, w_up_ref[...], 1, 1) * slope).astype(BF)
    share = dg(d_pre, w_down_ref[...], 1, 1) * inverse
    share_high = share.astype(BF)
    send_down[:, :C1] = back[:SPILL, :]
    send_down[:, C1:] = share_high[:SPILL, :]
    down = pltpu.make_async_remote_copy(
        send_down, recv_down, send_sem.at[1], recv_sem.at[1],
        device_id=before, device_id_type=MESH,
    )
    down.start()
    back_ref[:CORE, :] = back
    share_ref[:CORE, :] = share_high
    low_ref[:CORE, :] = (share - share_high.astype(F32)).astype(BF)
    low_ref[CORE:, :] = jnp.zeros((SPILL, C1), BF)
    grad_up_ref[...] = dg(activ, d_back, 0, 0)
    grad_down_ref[...] = dg(pooled, d_pre, 0, 0)
    down.wait()
    back_ref[CORE:, :] = recv_down[:, :C1]
    share_ref[CORE:, :] = recv_down[:, C1:]


def coarse_call(sums, counted, cot_sums, w_down, w_up):
    out = jax.ShapeDtypeStruct
    vmem = pl.BlockSpec(memory_space=pltpu.VMEM)
    return pl.pallas_call(
        coarse_kernel,
        in_specs=[vmem] * 5,
        out_specs=[vmem] * 5,
        out_shape=[
            out((TABLE, C1), BF),
            out((TABLE, C1), BF),
            out((TABLE, C1), BF),
            out((C2, C1), F32),
            out((C1, C2), F32),
        ],
        scratch_shapes=[
            pltpu.VMEM((SPILL, 2 * C1 + HALF), BF),
            pltpu.VMEM((SPILL, 2 * C1 + HALF), BF),
            pltpu.VMEM((SPILL, 2 * C1), BF),
            pltpu.VMEM((SPILL, 2 * C1), BF),
            pltpu.SemaphoreType.DMA((2,)),
            pltpu.SemaphoreType.DMA((2,)),
        ],
        compiler_params=pltpu.CompilerParams(
            collective_id=0, has_side_effects=True, vmem_limit_bytes=48 * 2**20
        ),
        name="coarse",
    )(sums, counted, cot_sums, w_down, w_up)


def backward_kernel(
    counts_ref, parent_ref, feats_ref, gain_ref, w_qkv_ref, w_out_ref, cot_ref,
    hidden_ref, att_ref, proj_ref, scale_ref, back_ref, share_ref, low_ref, raised_ref,
    result_ref, d_feats_ref, grad_qkv_ref, grad_out_ref,
    d_hidden_s, normed_s, d_att_s, d_proj_s, values_s, cots_s,
):
    step = pl.program_id(0)
    live = counts_ref[0]

    @pl.when(step == 0)
    def _():
        xhat, _ = norm_parts(feats_ref[...].astype(F32))
        normed = (xhat * gain_ref[...]).astype(BF)
        normed_s[...] = normed
        values = dg(normed, w_qkv_ref[:, 2 * C1 :], 1, 0).astype(BF)
        ones = jnp.where(iota((ROWS, HALF), 1) < 2, 1.0, 0.0).astype(BF)
        for half in range(2):
            values_s[half, :, :HALF] = values[:, half * HALF : (half + 1) * HALF]
            values_s[half, :, HALF:] = ones
        for one in range(PAIR):
            cots_s[one] = jnp.zeros((C1, ROWS), BF)
        local = parent_ref[...] - device_number() * CORE
        column = jnp.broadcast_to(local.astype(F32), (HALF, ROWS)).T[:, :1].astype(jnp.int32)
        member = (column == iota((ROWS, TABLE), 1)) & (iota((ROWS, TABLE), 0) < live)
        member_b = jnp.where(member, 1.0, 0.0).astype(BF)
        result_ref[...] = (
            hidden_ref[...].astype(F32) + dg(member_b, back_ref[...], 1, 0)
        ).astype(BF)
        d_hidden = (
            cot_ref[...].astype(F32)
            + dg(member_b, share_ref[...], 1, 0)
            + dg(member_b, low_ref[...], 1, 0)
        )
        d_hidden_s[...] = d_hidden
        d_hidden_b = d_hidden.astype(BF)
        grad_out_ref[...] = dg(att_ref[...], d_hidden_b, 1, 0)
        d_att_s[...] = dg(w_out_ref[...], d_hidden_b, 1, 1).astype(BF)

    half = step // (STEPS // 2)
    quarter = jnp.asarray(HD ** (-0.5), BF)
    for one in range(PAIR):
        head = step * PAIR + one
        start = pl.multiple_of(head * HD, HD)
        place = pl.multiple_of(lax.rem(head, HEADS // 2) * HD, HD)
        cot = (d_att_s[pl.ds(start, HD), :].astype(F32) * scale_ref[one, :1, :]).astype(BF)
        inner = -jnp.sum(
            cot.astype(F32) * att_ref[pl.ds(start, HD), :].astype(F32), axis=0, keepdims=True
        )
        high = inner.astype(BF).astype(F32)
        rows = iota((HD, ROWS), 0)
        cots_s[one, :HALF, :] = jnp.zeros((HALF, ROWS), BF)
        cots_s[one, pl.ds(place, HD), :] = cot
        cots_s[one, HALF : HALF + HD, :] = jnp.where(
            rows == 0, high, jnp.where(rows == 1, inner - high, 0.0)
        ).astype(BF)
        raised = raised_ref[one]
        d_scores = raised * dg(values_s[half], cots_s[one], 1, 0).astype(BF)
        d_proj_s[pl.ds(start, HD), :] = dg(
            proj_ref[pl.ds(C1 + start, HD), :] * quarter, d_scores, 1, 0
        ).astype(BF)
        d_proj_s[pl.ds(2 * C1 + start, HD), :] = dg(cot, raised, 1, 1).astype(BF)
        d_proj_s[pl.ds(C1 + start, HD), :] = dg(
            proj_ref[pl.ds(start, HD), :] * quarter, d_scores, 1, 1
        ).astype(BF)

    @pl.when(step == STEPS - 1)
    def _():
        grad_qkv_ref[...] = dg(normed_s[...], d_proj_s[...], 0, 1)
        d_normed = dg(w_qkv_ref[...], d_proj_s[...], 1, 0).T
        xhat, inverse = norm_parts(feats_ref[...].astype(F32))
        grown = d_normed * gain_ref[...]
        along = jnp.mean(grown * xhat, axis=-1, keepdims=True)
        d_wide = inverse * (grown - jnp.mean(grown, axis=-1, keepdims=True) - xhat * along)
        d_feats_ref[...] = (d_hidden_s[...] + d_wide).astype(BF)


def backward_call(
    counts, parent, feats, gain, w_qkv, w_out, cotangent,
    hidden, att, proj, scale, back, share, low, raised,
):
    out = jax.ShapeDtypeStruct
    return pl.pallas_call(
        backward_kernel,
        grid=(STEPS,),
        in_specs=[
            pl.BlockSpec(memory_space=pltpu.SMEM),
            whole((1, ROWS)),
            whole((ROWS, C1)),
            whole((1, C1)),
            whole((C1, 3 * C1)),
            whole((C1, C1)),
            whole((ROWS, C1)),
            whole((ROWS, C1)),
            whole((C1, ROWS)),
            whole((3 * C1, ROWS)),
            per_pair(8),
            whole((TABLE, C1)),
            whole((TABLE, C1)),
            whole((TABLE, C1)),
            per_pair(ROWS),
        ],
        out_specs=[
            whole((ROWS, C1)),
            whole((ROWS, C1)),
            whole((C1, 3 * C1)),
            whole((C1, C1)),
        ],
        out_shape=[
            out((ROWS, C1), BF),
            out((ROWS, C1), BF),
            out((C1, 3 * C1), F32),
            out((C1, C1), F32),
        ],
        scratch_shapes=[
            pltpu.VMEM((ROWS, C1), F32),
            pltpu.VMEM((ROWS, C1), BF),
            pltpu.VMEM((C1, ROWS), BF),
            pltpu.VMEM((3 * C1, ROWS), BF),
            pltpu.VMEM((2, ROWS, C1), BF),
            pltpu.VMEM((PAIR, C1, ROWS), BF),
        ],
        compiler_params=pltpu.CompilerParams(vmem_limit_bytes=56 * 2**20),
        name="backward",
    )(
        counts, parent, feats, gain, w_qkv, w_out, cotangent,
        hidden, att, proj, scale, back, share, low, raised,
    )


def per_device(feats, counts, parent, ln_gain, w_qkv, w_out, w_down, w_up, cotangent):
    parent_row = parent.reshape(1, ROWS)
    gain = ln_gain.reshape(1, C1)
    raised, proj, scale, att, hidden, sums, counted, cot_sums = forward_call(
        counts, parent_row, feats, gain, w_qkv, w_out, cotangent
    )
    back, share, low, grad_up, grad_down = coarse_call(sums, counted, cot_sums, w_down, w_up)
    result, d_feats, grad_qkv, grad_out = backward_call(
        counts, parent_row, feats, gain, w_qkv, w_out, cotangent,
        hidden, att, proj, scale, back, share, low, raised,
    )
    grad_qkv, grad_out, grad_down, grad_up = lax.psum(
        (grad_qkv, grad_out, grad_down, grad_up), ("pts", "grp")
    )
    return (result, d_feats, grad_qkv, grad_out, grad_down, grad_up)


def solution(mesh):
    rows = P(("pts", "grp"), None)
    line = P(("pts", "grp"))
    return jax.shard_map(
        per_device,
        mesh=mesh,
        in_specs=(rows, line, line, P(), P(), P(), P(), P(), rows),
        out_specs=(rows, rows, P(), P(), P(), P()),
        check_vma=False,
    )
```

time: 623 us -> 385 us (0.62)
  matrix products: 240 us -> 0 us
  Pallas kernels: 0 us -> 88.9 us
  other arithmetic: 70.1 us -> 0 us
  starting transfers between devices: 16.4 us -> 0.04 us
  waiting for transfers between devices: 255 us -> 266 us
  local copies, waits for them, and re-layouts: 21.4 us -> 14.2 us
    dot_general x62 -> x0, matrix products: 191 us -> none  [the longest x24 103 us: attend(): jnp.einsum('grs,gsd->grd', probs, values, preferred_element_type=jnp.floa...]
    pallas_call x0 -> x3, Pallas kernels: none -> 88.9 us  [the longest x1 41.1 us: backward_call(): pl.pallas_call(backward_kernel, grid=(STEPS,), in_specs=[pl.BlockSpec(mem...]
    reduce_sum x20 -> x0, other arithmetic: 50.4 us -> none  [the longest x8 28.1 us: attend(): raised = jnp.exp(scores - highest)]
    sub x8 -> x0, matrix products: 49.3 us -> none  [attend(): raised = jnp.exp(scores - highest)]
    ppermute x5 -> x0, starting transfers between devices: 16.4 us -> none  [shifted(): return lax.ppermute(block, axis, route)]
    psum x1, waiting for transfers between devices: 253 us -> 266 us  [per_device(): lax.psum((grad_qkv, grad_out, grad_down, grad_up), ('pts', 'grp'))]
    lt x16 -> x0, other arithmetic: 10.5 us -> none  [per_device(): live_rows = jnp.arange(rows_here, dtype=jnp.int32) < counts[0]]
    gather x2 -> x0, local copies, waits for them, and re-layouts: 8.45 us -> none  [the longest x1 4.98 us: per_device(): jnp.take(back_table, safe_parent, axis=0).astype(jnp.float32)]
  transfers between devices with their start and end apart: 6 -> 1, of which waited for: 2 -> 1; matrix products, arithmetic and copies ran while one was open for 51% -> 0% of each run, Pallas kernels for 0% -> 0%
where the time goes in v1:
time: 385 us; the launch traced here: 384 us
  waiting for transfers between devices  266 us (69%)
  Pallas kernels  88.9 us (23%)
  between operations  14.7 us (4%)
  local copies, waits for them, and re-layouts  14.2 us (4%)
    psum x1, waiting for transfers between devices, per_device(): lax.psum((grad_qkv, grad_out, grad_down, grad_up), ('pts', 'grp'))  266 us
    pallas_call x1, Pallas kernels, backward_call(): pl.pallas_call(backward_kernel, grid=(STEPS,), in_specs=[pl.BlockSpec(mem...  41.1 us
    pallas_call x1, Pallas kernels, forward_call(): pl.pallas_call(forward_kernel, grid=(STEPS,), in_specs=[pl.BlockSpec(memo...  37 us
    unnamed x20, local copies, waits for them, and re-layouts  14.2 us
    pallas_call x1, Pallas kernels, coarse_call(): pl.pallas_call(coarse_kernel, in_specs=[vmem] * 5, out_specs=[vmem] * 5,...  10.9 us
  transfers between devices with their start and end apart: 1, of which 1 were waited for; matrix products, arithmetic and copies ran while one was open for 0% of the time, Pallas kernels for 0%

profile of v1, /device:TPU:1, one launch (start us, length us, event | category | flops | bytes accessed | tf_op | source)
XLA Modules:
  0.0 384.4 jit_solution(11224880507030672362)
XLA Ops:
  7.2 0.0 all-reduce.3.cloned.1.call-start
  7.9 37.0 %forward.1 = (bf16[16,1024,1024]{2,1,0:T(8,128)(2,1)}, bf16[768,1024]{1,0:T(8,128)(2,1)}, f32[16,8,1024]{2,1,0:T(8,128)}, bf16[256,1024]{1,0:T(8,128)(2,1)}, bf1...) custom-call(s32[1]{0:T(128)S(6)} %copy.21.counts_ref, ...), custom_call_target="tpu_custom_call" | custom-call | tf_op jit(solution)/shard_map/forward/pallas_call | solution.py:141
  44.8 0.0 copy-start
  44.9 1.0 copy-done
  45.8 0.0 copy-start.1
  45.8 1.0 copy-done.1
  46.8 0.0 copy-start.2
  46.8 0.9 copy-done.2
  47.7 0.0 copy-start.3
  47.7 0.9 copy-done.3
  48.7 0.0 copy-start.4
  48.7 0.9 copy-done.4
  49.6 10.9 %coarse.1 = (bf16[320,256]{1,0:T(8,128)(2,1)S(1)}, bf16[320,256]{1,0:T(8,128)(2,1)S(1)}, bf16[320,256]{1,0:T(8,128)(2,1)S(1)}, f32[512,256]{1,0:T(8,128)}, f32[256,512]{1,0:T(8,128)}) custom-call(f32[320,256]{1,0:T(8,128)S(1)} %copy-done, f32[320,128]{1,0:T(8,128)S(1)} %copy-done.4, f32[320,256]{1,0:T(8,128)S(1)} %copy-done.1, ...), custom_call_target="tpu_custom_call" | custom-call | tf_op jit(solution)/shard_map/coarse/pallas_call | solution.py:264
  60.5 0.0 copy-start.5
  60.5 0.7 copy-done.5
  61.2 0.0 copy-start.6
  61.2 0.7 copy-done.6
  61.8 0.0 copy-start.7
  61.8 0.7 copy-done.7
  62.5 41.1 %backward.1 = (bf16[1024,256]{1,0:T(8,128)(2,1)}, bf16[1024,256]{1,0:T(8,128)(2,1)}, f32[256,768]{1,0:T(8,128)}, f32[256,256]{1,0:T(8,128)}) custom-call(s32[1]{0:T(128)S(6)} %copy.21.counts_ref, s32[1,1024]{1,0:T(1,128)} %bitcast.3, bf16[1024,256]{1,0:T(8,128)(2,1)} %feats_ref.3, f32[1,256]{1,0:T(1,128)} %bitcast.5, bf16[256,768]{1,0:T(8,128)(2,1)} %w_qkv_ref.3, ...), custom_call_target="tpu_custom_call" | custom-call | tf_op jit(solution)/shard_map/backward/pallas_call | solution.py:371
  103.6 0.0 all-reduce.3.cloned.1.call-update
  103.6 266.5 %all-reduce.3.cloned.1.call-done = (f32[256,768]{1,0:T(8,128)}, f32[256,256]{1,0:T(8,128)}, f32[256,512]{1,0:T(8,128)}, f32[512,256]{1,0:T(8,128)}) async-done(((f32[256,768]{1,0:T(8,128)}, f32[256,256]{1,0:T(8,128)}, f32[256,512]{1,0:T(8,128)}, f32[512,256]{1,0:T(8,128)}), (f32[256,768]{1,0:T(8,128)}, f32[256,256]{1,0:T(8,128)}, f32[256,512]{1,0:T(8,128)}, ...) | async-done | bytes 2097168 | tf_op jit(solution)/shard_map/psum | solution.py:430
  370.1 2.1 copy.22
  372.1 1.7 copy.23
  373.8 1.9 copy.24
  375.7 1.9 copy.25
Async XLA Ops:
  7.2 362.9 %all-reduce.3.cloned.1.call-start = ((), (), s32[]{:S(2)}) async-start(), calls=%async_computation | async-start | bytes 4194304 | tf_op jit(solution)/shard_map/psum | solution.py:430
  44.8 1.0 copy-start
  45.8 1.0 copy-start.1
  46.8 0.9 copy-start.2
  47.7 0.9 copy-start.3
  48.7 0.9 copy-start.4
  60.5 0.7 copy-start.5
  61.2 0.7 copy-start.6
  61.8 0.7 copy-start.7
Sparse Core Ops, SparseCore 0:
  103.7 266.2 all-reduce.2

commit v2 on v1

--- a/solution.py
+++ b/solution.py
@@ -1,5 +1,3 @@
-import functools
-
 import jax
 import jax.numpy as jnp
 from jax import lax
@@ -199,105 +197,201 @@
     return (other // lax.axis_size("grp"), lax.rem(other, lax.axis_size("grp")))
 
 
-def coarse_kernel(
-    sum_ref, count_ref, cot_sum_ref, w_down_ref, w_up_ref,
-    back_ref, share_ref, low_ref, grad_up_ref, grad_down_ref,
-    send_up, recv_up, send_down, recv_down, send_sem, recv_sem,
-):
-    after, before = neighbour(1), neighbour(-1)
-    barrier = pltpu.get_barrier_semaphore()
-    for other in (after, before):
-        pl.semaphore_signal(barrier, inc=1, device_id=other, device_id_type=MESH)
-    send_up[:, :C1] = sum_ref[CORE:, :].astype(BF)
-    send_up[:, C1 : 2 * C1] = cot_sum_ref[CORE:, :].astype(BF)
-    spilled = count_ref[CORE:, :]
-    high = spilled.astype(BF)
-    low = (spilled - high.astype(F32)).astype(BF)
-    send_up[:, 2 * C1 :] = jnp.where(iota((SPILL, HALF), 1) < HALF // 2, high, low)
-    pl.semaphore_wait(barrier, 2)
-    up = pltpu.make_async_remote_copy(
-        send_up, recv_up, send_sem.at[0], recv_sem.at[0],
-        device_id=after, device_id_type=MESH,
-    )
-    up.start()
-    up.wait()
-    got = recv_up[...].astype(F32)
-    count_in = got[:, 2 * C1 : 2 * C1 + 1] + got[:, 2 * C1 + HALF // 2 : 2 * C1 + HALF // 2 + 1]
-    own_sum = jnp.concatenate([sum_ref[:SPILL, :] + got[:, :C1], sum_ref[SPILL:CORE, :]], axis=0)
-    own_cot = jnp.concatenate(
-        [cot_sum_ref[:SPILL, :] + got[:, C1 : 2 * C1], cot_sum_ref[SPILL:CORE, :]], axis=0
-    )
-    counted = jnp.concatenate(
-        [count_ref[:SPILL, :1] + count_in, count_ref[SPILL:CORE, :1]], axis=0
-    )
-    inverse = 1.0 / jnp.maximum(counted, 1.0)
-    pooled = (own_sum * inverse).astype(BF)
-    pre = dg(pooled, w_down_ref[...], 1, 0)
-    value, slope = gelu_and_slope(pre)
-    activ = value.astype(BF)
-    back = dg(activ, w_up_ref[...], 1, 0).astype(BF)
-    d_back = own_cot.astype(BF)
-    d_pre = (dg(d_back, w_up_ref[...], 1, 1) * slope).astype(BF)
-    share = dg(d_pre, w_down_ref[...], 1, 1) * inverse
-    share_high = share.astype(BF)
-    send_down[:, :C1] = back[:SPILL, :]
-    send_down[:, C1:] = share_high[:SPILL, :]
-    down = pltpu.make_async_remote_copy(
-        send_down, recv_down, send_sem.at[1], recv_sem.at[1],
-        device_id=before, device_id_type=MESH,
-    )
-    down.start()
-    back_ref[:CORE, :] = back
-    share_ref[:CORE, :] = share_high
-    low_ref[:CORE, :] = (share - share_high.astype(F32)).astype(BF)
-    low_ref[CORE:, :] = jnp.zeros((SPILL, C1), BF)
-    grad_up_ref[...] = dg(activ, d_back, 0, 0)
-    grad_down_ref[...] = dg(pooled, d_pre, 0, 0)
-    down.wait()
-    back_ref[CORE:, :] = recv_down[:, :C1]
-    share_ref[CORE:, :] = recv_down[:, C1:]
-
-
-def coarse_call(sums, counted, cot_sums, w_down, w_up):
-    out = jax.ShapeDtypeStruct
-    vmem = pl.BlockSpec(memory_space=pltpu.VMEM)
-    return pl.pallas_call(
-        coarse_kernel,
-        in_specs=[vmem] * 5,
-        out_specs=[vmem] * 5,
-        out_shape=[
-            out((TABLE, C1), BF),
-            out((TABLE, C1), BF),
-            out((TABLE, C1), BF),
-            out((C2, C1), F32),
-            out((C1, C2), F32),
-        ],
-        scratch_shapes=[
-            pltpu.VMEM((SPILL, 2 * C1 + HALF), BF),
-            pltpu.VMEM((SPILL, 2 * C1 + HALF), BF),
-            pltpu.VMEM((SPILL, 2 * C1), BF),
-            pltpu.VMEM((SPILL, 2 * C1), BF),
-            pltpu.SemaphoreType.DMA((2,)),
-            pltpu.SemaphoreType.DMA((2,)),
-        ],
-        compiler_params=pltpu.CompilerParams(
-            collective_id=0, has_side_effects=True, vmem_limit_bytes=48 * 2**20
-        ),
-        name="coarse",
-    )(sums, counted, cot_sums, w_down, w_up)
+GROUP = 16
+UP_W = 2 * C1 + HALF
+EARLY_W = 2 * C1 + HALF
+EARLY_ROW, FIRST_ROW, SECOND_ROW, THIRD_ROW = 0, 5, 10, 13
+FIRST_W = 3 * HALF // 2
+LATE_W = 3 * HALF // 2
+
+
+class Places:
+    def __init__(self):
+        pts, self.y = lax.axis_index("pts"), lax.axis_index("grp")
+        self.core = lax.rem(pts, 2)
+        self.x = lax.rem(pts // 2, 4)
+        self.z = pts // 8
+        self.plane = self.x * 4 + self.y
+        self.line = self.z * 2 + self.core
+
+    def core_peer(self, j):
+        return (self.z * 8 + self.x * 2 + j, self.y)
+
+    def plane_peer(self, j):
+        return (self.z * 8 + (j // 4) * 2 + self.core, lax.rem(j, 4))
+
+    def column_peer(self, j):
+        return (j * 8 + self.x * 2 + self.core, self.y)
+
+    def line_peer(self, j):
+        return ((j // 2) * 8 + self.x * 2 + lax.rem(j, 2), self.y)
+
+
+class Exchange:
+    def __init__(self, sems, row, members, me, peer, src, dst):
+        self.send, self.recv = sems
+        self.row, self.members, self.me, self.peer = row, members, me, peer
+        self.src, self.dst = src, dst
+
+    def other(self, k):
+        return lax.rem(self.me + k, self.members)
+
+    def copy(self, k, slot):
+        return pltpu.make_async_remote_copy(
+            self.src(self.other(k)),
+            self.dst(slot),
+            self.send.at[self.row, k],
+            self.recv.at[self.row, slot],
+            device_id=self.peer(self.other(k)),
+            device_id_type=MESH,
+        )
+
+    def start(self):
+        def one(k, carry):
+            self.copy(k, self.me).start()
+            return carry
+
+        lax.fori_loop(1, self.members, one, 0)
+
+    def wait(self):
+        def one(k, carry):
+            copy = self.copy(k, self.other(k))
+            copy.wait_send()
+            copy.wait_recv()
+            return carry
+
+        lax.fori_loop(1, self.members, one, 0)
+
+
+def add_slots(first, ref, members, skip=None):
+    def one(j, total):
+        return total + ref[j].astype(F32)
+
+    return lax.fori_loop(0, members, one, first)
+
+
+class FiveStep:
+    def __init__(self, places, sems, row, data, pair, half, got, line, full):
+        core, plane = places.core, places.plane
+        self.places, self.data, self.pair, self.half = places, data, pair, half
+        self.got, self.line, self.full = got, line, full
+        self.stages = [
+            Exchange(sems, row, 2, core, places.core_peer,
+                     lambda j: data.at[j], lambda s: pair.at[s]),
+            Exchange(sems, row + 1, GROUP, plane, places.plane_peer,
+                     lambda j: half.at[j], lambda s: got.at[s]),
+            Exchange(sems, row + 2, 8, places.z, places.column_peer,
+                     lambda j: line.at[places.z], lambda s: line.at[s]),
+            Exchange(sems, row + 3, GROUP, plane, places.plane_peer,
+                     lambda j: full.at[core, plane], lambda s: full.at[core, s]),
+            Exchange(sems, row + 4, 2, core, places.core_peer,
+                     lambda j: full.at[core], lambda s: full.at[s]),
+        ]
+
+    def begin(self):
+        self.stages[0].start()
+
+    def advance(self, stage):
+        places = self.places
+        core, plane = places.core, places.plane
+        self.stages[stage].wait()
+        if stage == 0:
+            self.half[...] = (
+                self.data[core].astype(F32) + self.pair[1 - core].astype(F32)
+            ).astype(BF)
+            self.got[plane] = self.half[plane]
+        if stage == 1:
+            zero = jnp.zeros(self.got.shape[1:], F32)
+            self.line[places.z] = add_slots(zero, self.got, GROUP).astype(BF)
+        if stage == 2:
+            zero = jnp.zeros(self.got.shape[1:], F32)
+            self.full[core, plane] = add_slots(zero, self.line, 8).astype(BF)
+        if stage < 4:
+            self.stages[stage + 1].start()
+
+
+class ThreeStep:
+    def __init__(self, places, sems, row, data, got, line, full):
+        plane = places.plane
+        self.places, self.data, self.got = places, data, got
+        self.line, self.full = line, full
+        self.stages = [
+            Exchange(sems, row, GROUP, plane, places.plane_peer,
+                     lambda j: data.at[j], lambda s: got.at[s]),
+            Exchange(sems, row + 1, GROUP, places.line, places.line_peer,
+                     lambda j: line.at[places.line], lambda s: line.at[s]),
+            Exchange(sems, row + 2, GROUP, plane, places.plane_peer,
+                     lambda j: full.at[plane], lambda s: full.at[s]),
+        ]
+
+    def begin(self):
+        plane = self.places.plane
+        self.stages[0].start()
+        self.got[plane] = self.data[plane]
+
+    def advance(self, stage):
+        places = self.places
+        self.stages[stage].wait()
+        zero = jnp.zeros(self.got.shape[1:], F32)
+        if stage == 0:
+            self.line[places.line] = add_slots(zero, self.got, GROUP).astype(BF)
+        if stage == 1:
+            self.full[places.plane] = add_slots(zero, self.line, GROUP).astype(BF)
+        if stage < 2:
+            self.stages[stage + 1].start()
 
 
 def backward_kernel(
-    counts_ref, parent_ref, feats_ref, gain_ref, w_qkv_ref, w_out_ref, cot_ref,
-    hidden_ref, att_ref, proj_ref, scale_ref, back_ref, share_ref, low_ref, raised_ref,
-    result_ref, d_feats_ref, grad_qkv_ref, grad_out_ref,
-    d_hidden_s, normed_s, d_att_s, d_proj_s, values_s, cots_s,
+    counts_ref, parent_ref, feats_ref, gain_ref, w_qkv_ref, w_out_ref, w_down_ref, w_up_ref,
+    cot_ref, hidden_ref, att_ref, proj_ref, scale_ref, sum_ref, count_ref, cot_sum_ref,
+    raised_ref,
+    result_ref, d_feats_ref, early_ref, first_ref, second_ref, third_ref,
+    d_hidden_s, normed_s, d_att_s, d_proj_s, values_s, cots_s, member_s, back_s,
+    send_up, recv_up, send_down, recv_down,
+    e_data, e_pair, e_half, e_got, e_line, e_full,
+    f_data, f_pair, f_half, f_got, f_line, f_full,
+    s_data, s_got, s_line, s_full,
+    t_data, t_got, t_line, t_full,
+    near_send, near_recv, far_send, far_recv,
 ):
     step = pl.program_id(0)
     live = counts_ref[0]
+    places = Places()
+    sems = (far_send, far_recv)
+    early = FiveStep(places, sems, EARLY_ROW, e_data, e_pair, e_half, e_got, e_line, e_full)
+    first = FiveStep(places, sems, FIRST_ROW, f_data, f_pair, f_half, f_got, f_line, f_full)
+    second = ThreeStep(places, sems, SECOND_ROW, s_data, s_got, s_line, s_full)
+    third = ThreeStep(places, sems, THIRD_ROW, t_data, t_got, t_line, t_full)
 
     @pl.when(step == 0)
     def _():
+        after, before = neighbour(1), neighbour(-1)
+        barrier = pltpu.get_barrier_semaphore()
+        for other in (after, before):
+            pl.semaphore_signal(barrier, inc=1, device_id=other, device_id_type=MESH)
+
+        def greet(k, carry):
+            for other in (
+                places.plane_peer(lax.rem(places.plane + k, GROUP)),
+                places.line_peer(lax.rem(places.line + k, GROUP)),
+            ):
+                pl.semaphore_signal(barrier, inc=1, device_id=other, device_id_type=MESH)
+            return carry
+
+        lax.fori_loop(1, GROUP, greet, 0)
+        send_up[:, :C1] = sum_ref[CORE:, :].astype(BF)
+        send_up[:, C1 : 2 * C1] = cot_sum_ref[CORE:, :].astype(BF)
+        spilled = count_ref[CORE:, :]
+        high = spilled.astype(BF)
+        low = (spilled - high.astype(F32)).astype(BF)
+        send_up[:, 2 * C1 :] = jnp.where(iota((SPILL, HALF), 1) < HALF // 2, high, low)
+        pl.semaphore_wait(barrier, 2 * GROUP)
+        up = pltpu.make_async_remote_copy(
+            send_up, recv_up, near_send.at[0], near_recv.at[0],
+            device_id=after, device_id_type=MESH,
+        )
+        up.start()
+
         xhat, _ = norm_parts(feats_ref[...].astype(F32))
         normed = (xhat * gain_ref[...]).astype(BF)
         normed_s[...] = normed
@@ -311,19 +405,97 @@
         local = parent_ref[...] - device_number() * CORE
         column = jnp.broadcast_to(local.astype(F32), (HALF, ROWS)).T[:, :1].astype(jnp.int32)
         member = (column == iota((ROWS, TABLE), 1)) & (iota((ROWS, TABLE), 0) < live)
-        member_b = jnp.where(member, 1.0, 0.0).astype(BF)
-        result_ref[...] = (
-            hidden_ref[...].astype(F32) + dg(member_b, back_ref[...], 1, 0)
-        ).astype(BF)
+        member_s[...] = jnp.where(member, 1.0, 0.0).astype(BF)
+
+        up.wait()
+        got = recv_up[...].astype(F32)
+        count_in = (
+            got[:, 2 * C1 : 2 * C1 + 1] + got[:, 2 * C1 + HALF // 2 : 2 * C1 + HALF // 2 + 1]
+        )
+        own_sum = jnp.concatenate(
+            [sum_ref[:SPILL, :] + got[:, :C1], sum_ref[SPILL:CORE, :]], axis=0
+        )
+        own_cot = jnp.concatenate(
+            [cot_sum_ref[:SPILL, :] + got[:, C1 : 2 * C1], cot_sum_ref[SPILL:CORE, :]], axis=0
+        )
+        counted = jnp.concatenate(
+            [count_ref[:SPILL, :1] + count_in, count_ref[SPILL:CORE, :1]], axis=0
+        )
+        inverse = 1.0 / jnp.maximum(counted, 1.0)
+        pooled = (own_sum * inverse).astype(BF)
+        pre = dg(pooled, w_down_ref[...], 1, 0)
+        value, slope = gelu_and_slope(pre)
+        activ = value.astype(BF)
+        back = dg(activ, w_up_ref[...], 1, 0).astype(BF)
+        d_back = own_cot.astype(BF)
+        d_pre = (dg(d_back, w_up_ref[...], 1, 1) * slope).astype(BF)
+        share = dg(d_pre, w_down_ref[...], 1, 1) * inverse
+        share_high = share.astype(BF)
+        send_down[:, :C1] = back[:SPILL, :]
+        send_down[:, C1:] = share_high[:SPILL, :]
+        down = pltpu.make_async_remote_copy(
+            send_down, recv_down, near_send.at[1], near_recv.at[1],
+            device_id=before, device_id_type=MESH,
+        )
+        down.start()
+        share_low = (share - share_high.astype(F32)).astype(BF)
+        grad_up = dg(activ, d_back, 0, 0).astype(BF)
+        e_data[:, :, :, :C1] = grad_up.reshape(2, GROUP, 16, C1)
+        grad_down = dg(pooled, d_pre, 0, 0).astype(BF).reshape(GROUP, 16, C2)
+        for core in range(2):
+            e_data[core, :, :, C1 : 2 * C1] = grad_down[:, :, core * C1 : (core + 1) * C1]
+        back_s[:CORE, :] = back
+        down.wait()
+        back_s[CORE:, :] = recv_down[:, :C1]
+        share_in = recv_down[:, C1:]
+        member_b = member_s[...]
         d_hidden = (
             cot_ref[...].astype(F32)
-            + dg(member_b, share_ref[...], 1, 0)
-            + dg(member_b, low_ref[...], 1, 0)
+            + dg(member_b, jnp.concatenate([share_high, share_in], axis=0), 1, 0)
+            + dg(member_b[:, :CORE], share_low, 1, 0)
         )
         d_hidden_s[...] = d_hidden
         d_hidden_b = d_hidden.astype(BF)
-        grad_out_ref[...] = dg(att_ref[...], d_hidden_b, 1, 0)
+        grad_out = dg(att_ref[...], d_hidden_b, 1, 0).astype(BF).reshape(GROUP, 16, C1)
+        for core in range(2):
+            e_data[core, :, :, 2 * C1 :] = grad_out[:, :, core * HALF : (core + 1) * HALF]
+        early.begin()
         d_att_s[...] = dg(w_out_ref[...], d_hidden_b, 1, 1).astype(BF)
+
+    for stage in range(5):
+        @pl.when(step == stage + 1)
+        def _(stage=stage):
+            early.advance(stage)
+
+    def grad_columns(start, width):
+        return [
+            dg(normed_s[...], d_proj_s[part * C1 + start : part * C1 + start + width, :], 0, 1)
+            for part in range(3)
+        ]
+
+    @pl.when(step == 4)
+    def _():
+        grads = jnp.concatenate(grad_columns(0, HALF), axis=1).astype(BF)
+        for core in range(2):
+            f_data[core] = grads[:, core * FIRST_W : (core + 1) * FIRST_W].reshape(
+                GROUP, 16, FIRST_W
+            )
+        first.begin()
+
+    for stage in range(3):
+        @pl.when(step == stage + 5)
+        def _(stage=stage):
+            first.advance(stage)
+
+    @pl.when(step == 6)
+    def _():
+        grads = jnp.concatenate(grad_columns(HALF, HALF // 2), axis=1).astype(BF)
+        s_data[...] = grads.reshape(GROUP, 16, LATE_W)
+        second.begin()
+
+    @pl.when(step == 7)
+    def _():
+        second.advance(0)
 
     half = step // (STEPS // 2)
     quarter = jnp.asarray(HD ** (-0.5), BF)
@@ -354,20 +526,47 @@
 
     @pl.when(step == STEPS - 1)
     def _():
-        grad_qkv_ref[...] = dg(normed_s[...], d_proj_s[...], 0, 1)
+        grads = jnp.concatenate(grad_columns(HALF + HALF // 2, HALF // 2), axis=1).astype(BF)
+        t_data[...] = grads.reshape(GROUP, 16, LATE_W)
+        third.begin()
+        first.advance(3)
+        second.advance(1)
         d_normed = dg(w_qkv_ref[...], d_proj_s[...], 1, 0).T
+        third.advance(0)
         xhat, inverse = norm_parts(feats_ref[...].astype(F32))
         grown = d_normed * gain_ref[...]
         along = jnp.mean(grown * xhat, axis=-1, keepdims=True)
         d_wide = inverse * (grown - jnp.mean(grown, axis=-1, keepdims=True) - xhat * along)
         d_feats_ref[...] = (d_hidden_s[...] + d_wide).astype(BF)
+        third.advance(1)
+        result_ref[...] = (
+            hidden_ref[...].astype(F32) + dg(member_s[...], back_s[...], 1, 0)
+        ).astype(BF)
+        early_ref[...] = e_full[...]
+        first.advance(4)
+        first_ref[...] = f_full[...]
+        second.advance(2)
+        second_ref[...] = s_full[...]
+        third.advance(2)
+        third_ref[...] = t_full[...]
 
 
 def backward_call(
-    counts, parent, feats, gain, w_qkv, w_out, cotangent,
-    hidden, att, proj, scale, back, share, low, raised,
+    counts, parent, feats, gain, w_qkv, w_out, w_down, w_up, cotangent,
+    hidden, att, proj, scale, sums, counted, cot_sums, raised,
 ):
     out = jax.ShapeDtypeStruct
+    vmem = pltpu.VMEM
+    early, first, late = (
+        (2, GROUP, 16, EARLY_W), (2, GROUP, 16, FIRST_W), (GROUP, 16, LATE_W)
+    )
+
+    def five(shape):
+        return [
+            vmem(shape, BF), vmem(shape, BF), vmem(shape[1:], BF), vmem(shape[1:], BF),
+            vmem((8,) + shape[2:], BF), vmem(shape, BF),
+        ]
+
     return pl.pallas_call(
         backward_kernel,
         grid=(STEPS,),
@@ -378,42 +577,114 @@
             whole((1, C1)),
             whole((C1, 3 * C1)),
             whole((C1, C1)),
+            whole((C1, C2)),
+            whole((C2, C1)),
             whole((ROWS, C1)),
             whole((ROWS, C1)),
             whole((C1, ROWS)),
             whole((3 * C1, ROWS)),
             per_pair(8),
             whole((TABLE, C1)),
-            whole((TABLE, C1)),
+            whole((TABLE, HALF)),
             whole((TABLE, C1)),
             per_pair(ROWS),
         ],
         out_specs=[
             whole((ROWS, C1)),
             whole((ROWS, C1)),
-            whole((C1, 3 * C1)),
-            whole((C1, C1)),
+            whole(early),
+            whole(first),
+            whole(late),
+            whole(late),
         ],
         out_shape=[
             out((ROWS, C1), BF),
             out((ROWS, C1), BF),
-            out((C1, 3 * C1), F32),
-            out((C1, C1), F32),
+            out(early, BF),
+            out(first, BF),
+            out(late, BF),
+            out(late, BF),
         ],
         scratch_shapes=[
-            pltpu.VMEM((ROWS, C1), F32),
-            pltpu.VMEM((ROWS, C1), BF),
-            pltpu.VMEM((C1, ROWS), BF),
-            pltpu.VMEM((3 * C1, ROWS), BF),
-            pltpu.VMEM((2, ROWS, C1), BF),
-            pltpu.VMEM((PAIR, C1, ROWS), BF),
+            vmem((ROWS, C1), F32),
+            vmem((ROWS, C1), BF),
+            vmem((C1, ROWS), BF),
+            vmem((3 * C1, ROWS), BF),
+            vmem((2, ROWS, C1), BF),
+            vmem((PAIR, C1, ROWS), BF),
+            vmem((ROWS, TABLE), BF),
+            vmem((TABLE, C1), BF),
+            vmem((SPILL, UP_W), BF),
+            vmem((SPILL, UP_W), BF),
+            vmem((SPILL, 2 * C1), BF),
+            vmem((SPILL, 2 * C1), BF),
+        ]
+        + five(early)
+        + five(first)
+        + [vmem(late, BF)] * 8
+        + [
+            pltpu.SemaphoreType.DMA((2,)),
+            pltpu.SemaphoreType.DMA((2,)),
+            pltpu.SemaphoreType.DMA((16, GROUP)),
+            pltpu.SemaphoreType.DMA((16, GROUP)),
         ],
-        compiler_params=pltpu.CompilerParams(vmem_limit_bytes=56 * 2**20),
+        compiler_params=pltpu.CompilerParams(
+            collective_id=0, has_side_effects=True, vmem_limit_bytes=58 * 2**20
+        ),
         name="backward",
     )(
-        counts, parent, feats, gain, w_qkv, w_out, cotangent,
-        hidden, att, proj, scale, back, share, low, raised,
+        counts, parent, feats, gain, w_qkv, w_out, w_down, w_up, cotangent,
+        hidden, att, proj, scale, sums, counted, cot_sums, raised,
     )
+
+
+def finish_kernel(
+    result_ref, d_feats_ref, early_ref, first_ref, second_ref, third_ref,
+    result_out, d_feats_out, qkv_out, out_out, down_out, up_out,
+):
+    result_out[...] = result_ref[...]
+    d_feats_out[...] = d_feats_ref[...]
+    for core in range(2):
+        piece = early_ref[core]
+        up_out[core * C1 : (core + 1) * C1, :] = piece[:, :, :C1].reshape(C1, C1).astype(F32)
+        down_out[:, core * C1 : (core + 1) * C1] = (
+            piece[:, :, C1 : 2 * C1].reshape(C1, C1).astype(F32)
+        )
+        out_out[:, core * HALF : (core + 1) * HALF] = (
+            piece[:, :, 2 * C1 :].reshape(C1, HALF).astype(F32)
+        )
+    first = jnp.concatenate(
+        [first_ref[core].reshape(C1, FIRST_W).astype(F32) for core in range(2)], axis=1
+    )
+    second = second_ref[...].reshape(C1, LATE_W).astype(F32)
+    third = third_ref[...].reshape(C1, LATE_W).astype(F32)
+    quarter = HALF // 2
+    for part in range(3):
+        base = part * C1
+        qkv_out[:, base : base + HALF] = first[:, part * HALF : (part + 1) * HALF]
+        qkv_out[:, base + HALF : base + C1] = jnp.concatenate(
+            [
+                second[:, part * quarter : (part + 1) * quarter],
+                third[:, part * quarter : (part + 1) * quarter],
+            ],
+            axis=1,
+        )
+
+
+def finish_call(*parts):
+    shapes = [
+        ((ROWS, C1), BF), ((ROWS, C1), BF), ((C1, 3 * C1), F32), ((C1, C1), F32),
+        ((C1, C2), F32), ((C2, C1), F32),
+    ]
+    return pl.pallas_call(
+        finish_kernel,
+        grid=(1,),
+        in_specs=[whole(part.shape) for part in parts],
+        out_specs=[whole(shape) for shape, _ in shapes],
+        out_shape=[jax.ShapeDtypeStruct(shape, kind) for shape, kind in shapes],
+        compiler_params=pltpu.CompilerParams(vmem_limit_bytes=32 * 2**20),
+        name="finish",
+    )(*parts)
 
 
 def per_device(feats, counts, parent, ln_gain, w_qkv, w_out, w_down, w_up, cotangent):
@@ -422,15 +693,11 @@
     raised, proj, scale, att, hidden, sums, counted, cot_sums = forward_call(
         counts, parent_row, feats, gain, w_qkv, w_out, cotangent
     )
-    back, share, low, grad_up, grad_down = coarse_call(sums, counted, cot_sums, w_down, w_up)
-    result, d_feats, grad_qkv, grad_out = backward_call(
-        counts, parent_row, feats, gain, w_qkv, w_out, cotangent,
-        hidden, att, proj, scale, back, share, low, raised,
+    parts = backward_call(
+        counts, parent_row, feats, gain, w_qkv, w_out, w_down, w_up, cotangent,
+        hidden, att, proj, scale, sums, counted, cot_sums, raised,
     )
-    grad_qkv, grad_out, grad_down, grad_up = lax.psum(
-        (grad_qkv, grad_out, grad_down, grad_up), ("pts", "grp")
-    )
-    return (result, d_feats, grad_qkv, grad_out, grad_down, grad_up)
+    return tuple(finish_call(*parts))
 
 
 def solution(mesh):

time: 385 us -> 141 us (0.37)
  waiting for transfers between devices: 266 us -> 0 us
  Pallas kernels: 88.9 us -> 133 us
  between operations: 14.7 us -> 1.3 us
  local copies, waits for them, and re-layouts: 14.2 us -> 5.92 us
    psum x1 -> x0, waiting for transfers between devices: 266 us -> none  [per_device(): lax.psum((grad_qkv, grad_out, grad_down, grad_up), ('pts', 'grp'))]
    pallas_call x1, Pallas kernels: 41.1 us -> 94.4 us  [backward_call(): pl.pallas_call(backward_kernel, grid=(STEPS,), in_specs=[pl.BlockSpec(mem...]
    pallas_call x1, Pallas kernels: 10.9 us -> 1.79 us  [finish_call(): pl.pallas_call(finish_kernel, grid=(1,), in_specs=[whole(part.shape) for...]
    unnamed x20 -> x12, local copies, waits for them, and re-layouts: 14.2 us -> 5.92 us
  transfers between devices with their start and end apart: 1 -> 0, of which waited for: 1 -> 0; matrix products, arithmetic and copies ran while one was open for 0% -> 0% of each run, Pallas kernels for 0% -> 0%
where the time goes in v2:
time: 141 us; the launch traced here: 140 us
  Pallas kernels  133 us (94%)
  local copies, waits for them, and re-layouts  5.92 us (4%)
    pallas_call x1, Pallas kernels, backward_call(): pl.pallas_call(backward_kernel, grid=(STEPS,), in_specs=[pl.BlockSpec(mem...  94.4 us
    pallas_call x1, Pallas kernels, forward_call(): pl.pallas_call(forward_kernel, grid=(STEPS,), in_specs=[pl.BlockSpec(memo...  37 us
    unnamed x12, local copies, waits for them, and re-layouts  5.92 us

profile of v2, /device:TPU:1, one launch (start us, length us, event | category | flops | bytes accessed | tf_op | source)
XLA Modules:
  0.0 140.4 jit_solution(14858183171833712079)
XLA Ops:
  1.3 37.0 %forward.1 = (bf16[16,1024,1024]{2,1,0:T(8,128)(2,1)}, bf16[768,1024]{1,0:T(8,128)(2,1)}, f32[16,8,1024]{2,1,0:T(8,128)}, bf16[256,1024]{1,0:T(8,128)(2,1)}, bf1...) custom-call(s32[1]{0:T(128)S(6)} %copy.15.counts_ref, ...), custom_call_target="tpu_custom_call" | custom-call | tf_op jit(solution)/shard_map/forward/pallas_call | solution.py:139
  38.3 94.4 %backward.1 = (bf16[1024,256]{1,0:T(8,128)(2,1)}, bf16[1024,256]{1,0:T(8,128)(2,1)}, bf16[2,16,16,640]{3,2,1,0:T(8,128)(2,1)}, bf16[2,16,16,192]{3,2,1,0:T(8,128...) custom-call(s32[1]{0:T(128)S(6)} %copy.15.counts_ref, s32[1,1024]{1,0:T(1,128)} %bitcast.3, ...), custom_call_target="tpu_custom_call" | custom-call | tf_op jit(solution)/shard_map/backward/pallas_call | solution.py:570
  132.7 0.0 copy-start
  132.7 1.1 copy-done
  133.8 0.0 copy-start.1
  133.8 1.0 copy-done.1
  134.8 0.0 copy-start.2
  134.8 1.0 copy-done.2
  135.9 0.0 copy-start.3
  135.9 0.9 copy-done.3
  136.8 0.0 copy-start.4
  136.8 0.9 copy-done.4
  137.7 0.0 copy-start.5
  137.7 0.9 copy-done.5
  138.6 1.8 %finish.1 = (bf16[1024,256]{1,0:T(8,128)(2,1)}, bf16[1024,256]{1,0:T(8,128)(2,1)}, f32[256,768]{1,0:T(8,128)}, f32[256,256]{1,0:T(8,128)}, f32[256,512]{1,0:T(8,128)}, /*index=5*/f32[512,256]{1,0:T(8,128)}) custom-call(bf16[1024,256]{1,0:T(8,128)(2,1)S(1)} %copy-done.1, bf16[1024,256]{1,0:T(8,128)(2,1)S(1)} %copy-done.2, ...), custom_call_target="tpu_custom_call" | custom-call | tf_op jit(solution)/shard_map/finish/pallas_call | solution.py:679
Async XLA Ops:
  132.7 1.1 copy-start
  133.8 1.0 copy-start.1
  134.8 1.0 copy-start.2
  135.9 0.9 copy-start.3
  136.8 0.9 copy-start.4
  137.7 0.9 copy-start.5

commit v3 on v2

v3 whole, which is shorter than its diff:
```python
import jax
import jax.numpy as jnp
from jax import lax
from jax.experimental import pallas as pl
from jax.experimental.pallas import tpu as pltpu
from jax.sharding import PartitionSpec as P

HD = 16
HEADS = 16
ROWS = 1024
C1 = 256
C2 = 512
CORE = 256
SPILL = 64
TABLE = CORE + SPILL
PAIR = 2
STEPS = HEADS // PAIR
HALF = 128
SAFE_SCORE = 60.0
MESH = pl.DeviceIdType.MESH
BF = jnp.bfloat16
F32 = jnp.float32


def dg(left, right, left_dim, right_dim):
    return lax.dot_general(
        left,
        right,
        (((left_dim,), (right_dim,)), ((), ())),
        preferred_element_type=F32,
    )


def iota(shape, dim):
    return lax.broadcasted_iota(jnp.int32, shape, dim)


def norm_parts(wide):
    center = wide - jnp.mean(wide, axis=-1, keepdims=True)
    spread = jnp.mean(center * center, axis=-1, keepdims=True)
    inverse = lax.rsqrt(spread + 1e-05)
    return center * inverse, inverse


def device_number():
    return lax.axis_index("pts") * lax.axis_size("grp") + lax.axis_index("grp")


def whole(shape):
    return pl.BlockSpec(shape, lambda i, n=len(shape): (0,) * n)


def per_pair(rows):
    return pl.BlockSpec((PAIR, rows, ROWS), lambda i: (i, 0, 0))


def forward_kernel(
    counts_ref, feats_ref, gain_ref, w_qkv_ref,
    raised_ref, proj_ref, scale_ref, att_ref,
    keys_s, query_s, values_s, mixed_s, safe_s,
):
    step = pl.program_id(0)
    live = counts_ref[0]

    @pl.when(step == 0)
    def _():
        xhat, _ = norm_parts(feats_ref[...].astype(F32))
        normed = (xhat * gain_ref[...]).astype(BF)
        proj = dg(w_qkv_ref[...], normed, 0, 1).astype(BF)
        proj_ref[...] = proj
        keys = dg(normed, w_qkv_ref[:, C1 : 2 * C1], 1, 0).astype(BF)
        dead = (iota((ROWS, HALF), 0) >= live) & (iota((ROWS, HALF), 1) == 0)
        bias = jnp.where(dead, -1e30, 0.0).astype(BF)
        for half in range(2):
            keys_s[half, :, :HALF] = keys[:, half * HALF : (half + 1) * HALF]
            keys_s[half, :, HALF:] = bias
        ones = jnp.where(iota((HALF, ROWS), 0) == 0, 1.0, 0.0).astype(BF)
        for one in range(PAIR):
            query_s[one, HALF:, :] = ones
            values_s[one, HD:, :] = jnp.ones((HD, ROWS), BF)
        wide = proj[: 2 * C1, :].astype(F32)
        squares = jnp.sum((wide * wide).reshape(2, HEADS, HD, ROWS), axis=2)
        bound = jnp.max(squares[0]) * jnp.max(squares[1]) / HD
        safe_s[0] = (bound <= SAFE_SCORE * SAFE_SCORE).astype(jnp.int32)

    half = step // (STEPS // 2)
    for one in range(PAIR):
        head = step * PAIR + one
        start = pl.multiple_of(head * HD, HD)
        place = pl.multiple_of(lax.rem(head, HEADS // 2) * HD, HD)
        query_s[one, :HALF, :] = jnp.zeros((HALF, ROWS), BF)
        query_s[one, pl.ds(place, HD), :] = proj_ref[pl.ds(start, HD), :] * jnp.asarray(
            HD ** (-0.5), BF
        )
        values_s[one, :HD, :] = proj_ref[pl.ds(2 * C1 + start, HD), :]

    @pl.when(safe_s[0] == 1)
    def _():
        for one in range(PAIR):
            raised = jnp.exp(dg(keys_s[half], query_s[one], 1, 0)).astype(BF)
            raised_ref[one] = raised
            mixed_s[one] = dg(values_s[one], raised, 1, 0)

    @pl.when(safe_s[0] != 1)
    def _():
        for one in range(PAIR):
            scores = dg(keys_s[half], query_s[one], 1, 0)
            highest = jnp.max(scores, axis=0, keepdims=True)
            raised = jnp.exp(scores - highest).astype(BF)
            raised_ref[one] = raised
            mixed_s[one] = dg(values_s[one], raised, 1, 0)

    for one in range(PAIR):
        start = pl.multiple_of((step * PAIR + one) * HD, HD)
        scale = 1.0 / mixed_s[one, HD:, :]
        att_ref[pl.ds(start, HD), :] = (mixed_s[one, :HD, :] * scale).astype(BF)
        scale_ref[one] = scale[:8]


def forward_call(counts, feats, gain, w_qkv):
    out = jax.ShapeDtypeStruct
    return pl.pallas_call(
        forward_kernel,
        grid=(STEPS,),
        in_specs=[
            pl.BlockSpec(memory_space=pltpu.SMEM),
            whole((ROWS, C1)),
            whole((1, C1)),
            whole((C1, 3 * C1)),
        ],
        out_specs=[
            per_pair(ROWS),
            whole((3 * C1, ROWS)),
            per_pair(8),
            whole((C1, ROWS)),
        ],
        out_shape=[
            out((HEADS, ROWS, ROWS), BF),
            out((3 * C1, ROWS), BF),
            out((HEADS, 8, ROWS), F32),
            out((C1, ROWS), BF),
        ],
        scratch_shapes=[
            pltpu.VMEM((2, ROWS, C1), BF),
            pltpu.VMEM((PAIR, C1, ROWS), BF),
            pltpu.VMEM((PAIR, 2 * HD, ROWS), BF),
            pltpu.VMEM((PAIR, 2 * HD, ROWS), F32),
            pltpu.SMEM((1,), jnp.int32),
        ],
        compiler_params=pltpu.CompilerParams(vmem_limit_bytes=56 * 2**20),
        name="forward",
    )(counts, feats, gain, w_qkv)


def gelu_and_slope(pre):
    root = 0.7978845608028654
    square = pre * pre
    tanh = jnp.tanh(root * (pre + 0.044715 * (square * pre)))
    value = pre * (0.5 * (1.0 + tanh))
    slope = 0.5 * (1.0 + tanh) + 0.5 * pre * (1.0 - tanh * tanh) * root * (
        1.0 + 3 * 0.044715 * square
    )
    return value, slope


def neighbour(distance):
    devices = lax.axis_size("pts") * lax.axis_size("grp")
    other = lax.rem(device_number() + distance + devices, devices)
    return (other // lax.axis_size("grp"), lax.rem(other, lax.axis_size("grp")))


GROUP = 16
UP_W = 2 * C1 + HALF
EARLY_W = 2 * C1 + HALF
EARLY_ROW, FIRST_ROW, SECOND_ROW, THIRD_ROW = 0, 5, 10, 15
FIRST_HEADS, SECOND_HEADS, THIRD_HEADS = 8, 4, 4
FIRST_W, SECOND_W, THIRD_W = (FIRST_HEADS * 24, SECOND_HEADS * 24, THIRD_HEADS * 48)
SERVICES = (
    (1, "early", 0), (5, "early", 1), (9, "early", 2), (13, "early", 3),
    (8, "first", -1), (9, "first", 0), (13, "first", 1),
    (12, "second", -1), (13, "second", 0),
)


class Places:
    def __init__(self):
        pts, self.y = lax.axis_index("pts"), lax.axis_index("grp")
        self.core = lax.rem(pts, 2)
        self.x = lax.rem(pts // 2, 4)
        self.z = pts // 8
        self.plane = self.x * 4 + self.y
        self.line = self.z * 2 + self.core

    def core_peer(self, j):
        return (self.z * 8 + self.x * 2 + j, self.y)

    def plane_peer(self, j):
        return (self.z * 8 + (j // 4) * 2 + self.core, lax.rem(j, 4))

    def column_peer(self, j):
        return (j * 8 + self.x * 2 + self.core, self.y)

    def line_peer(self, j):
        return ((j // 2) * 8 + self.x * 2 + lax.rem(j, 2), self.y)


class Exchange:
    def __init__(self, sems, row, members, me, peer, src, slots):
        self.send, self.recv = sems
        self.row, self.members, self.me, self.peer = row, members, me, peer
        self.src, self.slots = src, slots

    def copy(self, src, dst, k):
        return pltpu.make_async_remote_copy(
            src,
            dst,
            self.send.at[self.row],
            self.recv.at[self.row],
            device_id=self.peer(lax.rem(self.me + k, self.members)),
            device_id_type=MESH,
        )

    def start(self):
        for k in range(1, self.members):
            src = self.src(lax.rem(self.me + k, self.members))
            self.copy(src, self.slots.at[self.me], k).start()

    def wait(self):
        others = self.slots.at[pl.ds(0, self.members - 1)]
        copy = self.copy(others, others, 1)
        copy.wait_send()
        copy.wait_recv()


def add_slots(ref):
    return jnp.sum(ref[...].astype(F32), axis=0).astype(BF)


class FiveStep:
    def __init__(self, places, sems, row, data, pair, half, got, line, full):
        core, plane = places.core, places.plane
        self.places, self.data, self.pair, self.half = places, data, pair, half
        self.got, self.line, self.full = got, line, full
        self.stages = [
            Exchange(sems, row, 2, core, places.core_peer,
                     lambda j: data.at[j], pair),
            Exchange(sems, row + 1, GROUP, plane, places.plane_peer,
                     lambda j: half.at[j], got),
            Exchange(sems, row + 2, 8, places.z, places.column_peer,
                     lambda j: line.at[places.z], line),
            Exchange(sems, row + 3, GROUP, plane, places.plane_peer,
                     lambda j: full.at[core, plane], full.at[core]),
            Exchange(sems, row + 4, 2, core, places.core_peer,
                     lambda j: full.at[core], full),
        ]

    def begin(self):
        self.stages[0].start()

    def advance(self, stage):
        places = self.places
        core, plane = places.core, places.plane
        self.stages[stage].wait()
        if stage == 0:
            self.half[...] = (
                self.data[core].astype(F32) + self.pair[1 - core].astype(F32)
            ).astype(BF)
            self.got[plane] = self.half[plane]
        if stage == 1:
            self.line[places.z] = add_slots(self.got)
        if stage == 2:
            self.full[core, plane] = add_slots(self.line)
        if stage < 4:
            self.stages[stage + 1].start()


class ThreeStep:
    def __init__(self, places, sems, row, data, got, line, full):
        plane = places.plane
        self.places, self.data, self.got = places, data, got
        self.line, self.full = line, full
        self.stages = [
            Exchange(sems, row, GROUP, plane, places.plane_peer,
                     lambda j: data.at[j], got),
            Exchange(sems, row + 1, GROUP, places.line, places.line_peer,
                     lambda j: line.at[places.line], line),
            Exchange(sems, row + 2, GROUP, plane, places.plane_peer,
                     lambda j: full.at[plane], full),
        ]

    def begin(self):
        plane = self.places.plane
        self.stages[0].start()
        self.got[plane] = self.data[plane]

    def advance(self, stage):
        places = self.places
        self.stages[stage].wait()
        if stage == 0:
            self.line[places.line] = add_slots(self.got)
        if stage == 1:
            self.full[places.plane] = add_slots(self.line)
        if stage < 2:
            self.stages[stage + 1].start()


def backward_kernel(
    counts_ref, parent_ref, feats_ref, gain_ref, w_qkv_ref, w_out_ref, w_down_ref, w_up_ref,
    cot_ref, att_ref, scale_ref, proj_hbm, raised_hbm,
    result_ref, d_feats_ref, early_ref, first_ref, second_ref, third_ref,
    proj_ref, raised_s, hidden_s, sum_s,
    d_hidden_s, normed_s, across_s, d_att_s, d_proj_s, values_s, cots_s, member_s, back_s,
    send_up, recv_up, send_down, recv_down,
    e_data, e_pair, e_half, e_got, e_line, e_full,
    f_data, f_pair, f_half, f_got, f_line, f_full,
    s_data, s_pair, s_half, s_got, s_line, s_full,
    t_data, t_got, t_line, t_full,
    near_send, near_recv, far_send, far_recv, load_sem,
):
    step = pl.program_id(0)
    live = counts_ref[0]
    places = Places()
    sems = (far_send, far_recv)
    early = FiveStep(places, sems, EARLY_ROW, e_data, e_pair, e_half, e_got, e_line, e_full)
    first = FiveStep(places, sems, FIRST_ROW, f_data, f_pair, f_half, f_got, f_line, f_full)
    second = FiveStep(places, sems, SECOND_ROW, s_data, s_pair, s_half, s_got, s_line, s_full)
    third = ThreeStep(places, sems, THIRD_ROW, t_data, t_got, t_line, t_full)
    chunks = {"early": early, "first": first, "second": second, "third": third}
    load_proj = pltpu.make_async_copy(proj_hbm, proj_ref, load_sem.at[2])

    def load_raised(at):
        slot = lax.rem(at, 2)
        return pltpu.make_async_copy(
            raised_hbm.at[pl.ds(at * PAIR, PAIR)], raised_s.at[slot], load_sem.at[slot]
        )

    @pl.when(step == 0)
    def _():
        after, before = neighbour(1), neighbour(-1)
        barrier = pltpu.get_barrier_semaphore()
        for other in (after, before):
            pl.semaphore_signal(barrier, inc=1, device_id=other, device_id_type=MESH)
        for k in range(1, GROUP):
            for other in (
                places.plane_peer(lax.rem(places.plane + k, GROUP)),
                places.line_peer(lax.rem(places.line + k, GROUP)),
            ):
                pl.semaphore_signal(barrier, inc=1, device_id=other, device_id_type=MESH)
        load_proj.start()
        load_raised(0).start()

        attended = att_ref[...].T
        hidden = (
            feats_ref[...].astype(F32) + dg(attended, w_out_ref[...], 1, 0)
        ).astype(BF)
        hidden_s[...] = hidden
        local = parent_ref[...] - device_number() * CORE
        member = (local == iota((TABLE, ROWS), 0)) & (iota((TABLE, ROWS), 1) < live)
        member_f = jnp.where(member, 1.0, 0.0)
        counted = jnp.sum(member_f, axis=1, keepdims=True)
        sum_s[:, :C1] = dg(member_f.astype(BF), hidden, 1, 0)
        sum_s[:, C1 : 2 * C1] = dg(member_f.astype(BF), cot_ref[...], 1, 0)
        sum_s[:, 2 * C1 :] = jnp.broadcast_to(counted, (TABLE, HALF))
        for buf, rows in ((send_up, slice(CORE, TABLE)), (send_down, slice(0, SPILL))):
            buf[:, : 2 * C1] = sum_s[rows, : 2 * C1].astype(BF)
            count = sum_s[rows, 2 * C1 :]
            high = count.astype(BF)
            low = (count - high.astype(F32)).astype(BF)
            buf[:, 2 * C1 :] = jnp.where(iota((SPILL, HALF), 1) < HALF // 2, high, low)
        pl.semaphore_wait(barrier, 2 * GROUP)
        up = pltpu.make_async_remote_copy(
            send_up, recv_up, near_send.at[0], near_recv.at[0],
            device_id=after, device_id_type=MESH,
        )
        down = pltpu.make_async_remote_copy(
            send_down, recv_down, near_send.at[1], near_recv.at[1],
            device_id=before, device_id_type=MESH,
        )
        up.start()
        down.start()

        xhat, _ = norm_parts(feats_ref[...].astype(F32))
        normed = (xhat * gain_ref[...]).astype(BF)
        normed_s[...] = normed
        across_s[...] = normed.T
        values = dg(normed, w_qkv_ref[:, 2 * C1 :], 1, 0).astype(BF)
        ones = jnp.where(iota((ROWS, HALF), 1) < 2, 1.0, 0.0).astype(BF)
        for half in range(2):
            values_s[half, :, :HALF] = values[:, half * HALF : (half + 1) * HALF]
            values_s[half, :, HALF:] = ones
        for one in range(PAIR):
            cots_s[one] = jnp.zeros((C1, ROWS), BF)
        column = jnp.broadcast_to(local.astype(F32), (HALF, ROWS)).T[:, :1].astype(jnp.int32)
        member = (column == iota((ROWS, TABLE), 1)) & (iota((ROWS, TABLE), 0) < live)
        member_s[...] = jnp.where(member, 1.0, 0.0).astype(BF)

        up.wait()
        down.wait()
        sums = []
        for buf, rows in ((recv_up, slice(0, SPILL)), (recv_down, slice(CORE, TABLE))):
            got = buf[...].astype(F32)
            count_in = (
                got[:, 2 * C1 : 2 * C1 + 1]
                + got[:, 2 * C1 + HALF // 2 : 2 * C1 + HALF // 2 + 1]
            )
            sums.append(
                (
                    sum_s[rows, :C1] + got[:, :C1],
                    sum_s[rows, C1 : 2 * C1] + got[:, C1 : 2 * C1],
                    sum_s[rows, 2 * C1 : 2 * C1 + 1] + count_in,
                )
            )
        middle = slice(SPILL, CORE)
        sums.insert(
            1,
            (
                sum_s[middle, :C1],
                sum_s[middle, C1 : 2 * C1],
                sum_s[middle, 2 * C1 : 2 * C1 + 1],
            ),
        )
        own_sum, own_cot, counted = [
            jnp.concatenate([piece[n] for piece in sums], axis=0) for n in range(3)
        ]
        inverse = 1.0 / jnp.maximum(counted, 1.0)
        pooled = (own_sum * inverse).astype(BF)
        pre = dg(pooled, w_down_ref[...], 1, 0)
        value, slope = gelu_and_slope(pre)
        activ = value.astype(BF)
        back_s[...] = dg(activ, w_up_ref[...], 1, 0).astype(BF)
        d_back = own_cot.astype(BF)
        d_pre = (dg(d_back, w_up_ref[...], 1, 1) * slope).astype(BF)
        share = dg(d_pre, w_down_ref[...], 1, 1) * inverse
        share_high = share.astype(BF)
        share_low = (share - share_high.astype(F32)).astype(BF)
        grad_up = dg(activ[:CORE], d_back[:CORE], 0, 0).astype(BF)
        e_data[:, :, :, :C1] = grad_up.reshape(2, GROUP, 16, C1)
        grad_down = dg(pooled[:CORE], d_pre[:CORE], 0, 0).astype(BF).reshape(GROUP, 16, C2)
        for core in range(2):
            e_data[core, :, :, C1 : 2 * C1] = grad_down[:, :, core * C1 : (core + 1) * C1]
        member_b = member_s[...]
        d_hidden = (
            cot_ref[...].astype(F32)
            + dg(member_b, share_high, 1, 0)
            + dg(member_b, share_low, 1, 0)
        )
        d_hidden_s[...] = d_hidden
        d_hidden_b = d_hidden.astype(BF)
        grad_out = dg(att_ref[...], d_hidden_b, 1, 0).astype(BF).reshape(GROUP, 16, C1)
        for core in range(2):
            e_data[core, :, :, 2 * C1 :] = grad_out[:, :, core * HALF : (core + 1) * HALF]
        early.begin()
        d_att_s[...] = dg(w_out_ref[...], d_hidden_b, 1, 1).astype(BF)
        load_proj.wait()

    @pl.when(step < STEPS - 1)
    def _():
        load_raised(step + 1).start()

    load_raised(step).wait()

    def grad_columns(head, heads):
        rows = [
            d_proj_s[part * C1 + head * HD : part * C1 + (head + heads) * HD, :]
            for part in range(3)
        ]
        return dg(across_s[...], jnp.concatenate(rows, axis=0), 1, 1).astype(BF)

    def fill_halves(data, head, heads):
        grads = grad_columns(head, heads)
        width = 3 * heads * HD // 2
        for core in range(2):
            data[core] = grads[:, core * width : (core + 1) * width].reshape(GROUP, 16, width)

    def serve(name, stage):
        if stage >= 0:
            chunks[name].advance(stage)
            return
        if name == "first":
            fill_halves(f_data, 0, FIRST_HEADS)
        else:
            fill_halves(s_data, FIRST_HEADS, SECOND_HEADS)
        chunks[name].begin()

    half = step // (STEPS // 2)
    quarter = jnp.asarray(HD ** (-0.5), BF)
    for one in range(PAIR):
        for turn, name, stage in SERVICES:
            if turn % PAIR == one:
                @pl.when(step == turn // PAIR)
                def _(name=name, stage=stage):
                    serve(name, stage)

        head = step * PAIR + one
        start = pl.multiple_of(head * HD, HD)
        place = pl.multiple_of(lax.rem(head, HEADS // 2) * HD, HD)
        cot = (d_att_s[pl.ds(start, HD), :].astype(F32) * scale_ref[one, :1, :]).astype(BF)
        inner = -jnp.sum(
            cot.astype(F32) * att_ref[pl.ds(start, HD), :].astype(F32), axis=0, keepdims=True
        )
        high = inner.astype(BF).astype(F32)
        rows = iota((HD, ROWS), 0)
        cots_s[one, :HALF, :] = jnp.zeros((HALF, ROWS), BF)
        cots_s[one, pl.ds(place, HD), :] = cot
        cots_s[one, HALF : HALF + HD, :] = jnp.where(
            rows == 0, high, jnp.where(rows == 1, inner - high, 0.0)
        ).astype(BF)
        raised = raised_s[lax.rem(step, 2), one]
        d_scores = raised * dg(values_s[half], cots_s[one], 1, 0).astype(BF)
        d_proj_s[pl.ds(start, HD), :] = dg(
            proj_ref[pl.ds(C1 + start, HD), :] * quarter, d_scores, 1, 0
        ).astype(BF)
        d_proj_s[pl.ds(2 * C1 + start, HD), :] = dg(cot, raised, 1, 1).astype(BF)
        d_proj_s[pl.ds(C1 + start, HD), :] = dg(
            proj_ref[pl.ds(start, HD), :] * quarter, d_scores, 1, 1
        ).astype(BF)

    @pl.when(step == STEPS - 1)
    def _():
        grads = grad_columns(FIRST_HEADS + SECOND_HEADS, THIRD_HEADS)
        t_data[...] = grads.reshape(GROUP, 16, THIRD_W)
        third.begin()
        early.advance(4)
        first.advance(2)
        d_normed = dg(w_qkv_ref[...], d_proj_s[...], 1, 0).T
        second.advance(1)
        xhat, inverse = norm_parts(feats_ref[...].astype(F32))
        grown = d_normed * gain_ref[...]
        along = jnp.mean(grown * xhat, axis=-1, keepdims=True)
        d_wide = inverse * (grown - jnp.mean(grown, axis=-1, keepdims=True) - xhat * along)
        d_feats_ref[...] = (d_hidden_s[...] + d_wide).astype(BF)
        third.advance(0)
        first.advance(3)
        result_ref[...] = (
            hidden_s[...].astype(F32) + dg(member_s[...], back_s[...], 1, 0)
        ).astype(BF)
        early_ref[...] = e_full[...]
        second.advance(2)
        third.advance(1)
        first.advance(4)
        first_ref[...] = f_full[...]
        second.advance(3)
        second.advance(4)
        second_ref[...] = s_full[...]
        third.advance(2)
        third_ref[...] = t_full[...]


def backward_call(
    counts, parent, feats, gain, w_qkv, w_out, w_down, w_up, cotangent,
    att, scale, proj, raised,
):
    out = jax.ShapeDtypeStruct
    vmem = pltpu.VMEM
    early, first, second, third = (
        (2, GROUP, 16, EARLY_W),
        (2, GROUP, 16, FIRST_W),
        (2, GROUP, 16, SECOND_W),
        (GROUP, 16, THIRD_W),
    )

    def five(shape):
        return [
            vmem(shape, BF), vmem(shape, BF), vmem(shape[1:], BF), vmem(shape[1:], BF),
            vmem((8,) + shape[2:], BF), vmem(shape, BF),
        ]

    return pl.pallas_call(
        backward_kernel,
        grid=(STEPS,),
        in_specs=[
            pl.BlockSpec(memory_space=pltpu.SMEM),
            whole((1, ROWS)),
            whole((ROWS, C1)),
            whole((1, C1)),
            whole((C1, 3 * C1)),
            whole((C1, C1)),
            whole((C1, C2)),
            whole((C2, C1)),
            whole((ROWS, C1)),
            whole((C1, ROWS)),
            per_pair(8),
            pl.BlockSpec(memory_space=pl.ANY),
            pl.BlockSpec(memory_space=pl.ANY),
        ],
        out_specs=[
            whole((ROWS, C1)),
            whole((ROWS, C1)),
            whole(early),
            whole(first),
            whole(second),
            whole(third),
        ],
        out_shape=[
            out((ROWS, C1), BF),
            out((ROWS, C1), BF),
            out(early, BF),
            out(first, BF),
            out(second, BF),
            out(third, BF),
        ],
        scratch_shapes=[
            vmem((3 * C1, ROWS), BF),
            vmem((2, PAIR, ROWS, ROWS), BF),
            vmem((ROWS, C1), BF),
            vmem((TABLE, UP_W), F32),
            vmem((ROWS, C1), F32),
            vmem((ROWS, C1), BF),
            vmem((C1, ROWS), BF),
            vmem((C1, ROWS), BF),
            vmem((3 * C1, ROWS), BF),
            vmem((2, ROWS, C1), BF),
            vmem((PAIR, C1, ROWS), BF),
            vmem((ROWS, TABLE), BF),
            vmem((TABLE, C1), BF),
            vmem((SPILL, UP_W), BF),
            vmem((SPILL, UP_W), BF),
            vmem((SPILL, UP_W), BF),
            vmem((SPILL, UP_W), BF),
        ]
        + five(early)
        + five(first)
        + five(second)
        + [vmem(third, BF)] * 4
        + [
            pltpu.SemaphoreType.DMA((2,)),
            pltpu.SemaphoreType.DMA((2,)),
            pltpu.SemaphoreType.DMA((18,)),
            pltpu.SemaphoreType.DMA((18,)),
            pltpu.SemaphoreType.DMA((3,)),
        ],
        compiler_params=pltpu.CompilerParams(
            collective_id=0, has_side_effects=True, vmem_limit_bytes=58 * 2**20
        ),
        name="backward",
    )(
        counts, parent, feats, gain, w_qkv, w_out, w_down, w_up, cotangent,
        att, scale, proj, raised,
    )


def finish_kernel(
    result_ref, d_feats_ref, early_ref, first_ref, second_ref, third_ref,
    result_out, d_feats_out, qkv_out, out_out, down_out, up_out,
):
    result_out[...] = result_ref[...]
    d_feats_out[...] = d_feats_ref[...]
    for core in range(2):
        piece = early_ref[core]
        up_out[core * C1 : (core + 1) * C1, :] = piece[:, :, :C1].reshape(C1, C1).astype(F32)
        down_out[:, core * C1 : (core + 1) * C1] = (
            piece[:, :, C1 : 2 * C1].reshape(C1, C1).astype(F32)
        )
        out_out[:, core * HALF : (core + 1) * HALF] = (
            piece[:, :, 2 * C1 :].reshape(C1, HALF).astype(F32)
        )
    low, high = [
        jnp.concatenate([ref[core].reshape(C1, width).astype(F32) for core in range(2)], axis=1)
        for ref, width in ((first_ref, FIRST_W), (second_ref, SECOND_W))
    ]
    last = third_ref[...].reshape(C1, THIRD_W).astype(F32)
    for part in range(3):
        qkv_out[:, part * C1 : (part + 1) * C1] = jnp.concatenate(
            [
                piece[:, part * heads * HD : (part + 1) * heads * HD]
                for piece, heads in (
                    (low, FIRST_HEADS), (high, SECOND_HEADS), (last, THIRD_HEADS)
                )
            ],
            axis=1,
        )


def finish_call(*parts):
    shapes = [
        ((ROWS, C1), BF), ((ROWS, C1), BF), ((C1, 3 * C1), F32), ((C1, C1), F32),
        ((C1, C2), F32), ((C2, C1), F32),
    ]
    return pl.pallas_call(
        finish_kernel,
        grid=(1,),
        in_specs=[whole(part.shape) for part in parts],
        out_specs=[whole(shape) for shape, _ in shapes],
        out_shape=[jax.ShapeDtypeStruct(shape, kind) for shape, kind in shapes],
        compiler_params=pltpu.CompilerParams(vmem_limit_bytes=60 * 2**20),
        name="finish",
    )(*parts)


def per_device(feats, counts, parent, ln_gain, w_qkv, w_out, w_down, w_up, cotangent):
    parent_row = parent.reshape(1, ROWS)
    gain = ln_gain.reshape(1, C1)
    raised, proj, scale, att = forward_call(counts, feats, gain, w_qkv)
    parts = backward_call(
        counts, parent_row, feats, gain, w_qkv, w_out, w_down, w_up, cotangent,
        att, scale, proj, raised,
    )
    return tuple(finish_call(*parts))


def solution(mesh):
    rows = P(("pts", "grp"), None)
    line = P(("pts", "grp"))
    return jax.shard_map(
        per_device,
        mesh=mesh,
        in_specs=(rows, line, line, P(), P(), P(), P(), P(), rows),
        out_specs=(rows, rows, P(), P(), P(), P()),
        check_vma=False,
    )
```

time: 141 us -> 113 us (0.80)
  Pallas kernels: 133 us -> 112 us
  local copies, waits for them, and re-layouts: 5.92 us -> 0 us
    pallas_call x1, Pallas kernels: 94.4 us -> 73.3 us  [backward_call(): pl.pallas_call(backward_kernel, grid=(STEPS,), in_specs=[pl.BlockSpec(mem...]
    unnamed x12 -> x0, local copies, waits for them, and re-layouts: 5.92 us -> none
    pallas_call x1, Pallas kernels: 37 us -> 35.3 us  [forward_call(): pl.pallas_call(forward_kernel, grid=(STEPS,), in_specs=[pl.BlockSpec(memo...]
    pallas_call x1, Pallas kernels: 1.79 us -> 3.37 us  [finish_call(): pl.pallas_call(finish_kernel, grid=(1,), in_specs=[whole(part.shape) for...]
where the time goes in v3:
time: 113 us
  Pallas kernels  112 us (99%)
  between operations  1.29 us (1%)
    pallas_call x1, Pallas kernels, backward_call(): pl.pallas_call(backward_kernel, grid=(STEPS,), in_specs=[pl.BlockSpec(mem...  73.3 us
    pallas_call x1, Pallas kernels, forward_call(): pl.pallas_call(forward_kernel, grid=(STEPS,), in_specs=[pl.BlockSpec(memo...  35.3 us
    pallas_call x1, Pallas kernels, finish_call(): pl.pallas_call(finish_kernel, grid=(1,), in_specs=[whole(part.shape) for...  3.37 us

profile of v3, /device:TPU:1, one launch (start us, length us, event | category | flops | bytes accessed | tf_op | source)
XLA Modules:
  0.0 113.2 jit_solution(913926858327064147)
XLA Ops:
  1.3 35.3 %forward.1 = (bf16[16,1024,1024]{2,1,0:T(8,128)(2,1)}, bf16[768,1024]{1,0:T(8,128)(2,1)}, f32[16,8,1024]{2,1,0:T(8,128)}, bf16[256,1024]{1,0:T(8,128)(2,1)}) custom-call(s32[1]{0:T(128)S(6)} %copy.15.counts_ref, bf16[1024,256]{1,0:T(8,128)(2,1)} %feats_ref.3, f32[1,256]{1,0:T(1,128)} %bitcast.2, bf16[256,768]{1,0:T(8,128)(2,1)} %w_qkv_ref.3), custom_call_target="tpu_custom_call" | custom-call | tf_op jit(solution)/shard_map/forward/pallas_call | solution.py:122
  36.6 73.3 %backward.1 = (bf16[1024,256]{1,0:T(8,128)(2,1)}, bf16[1024,256]{1,0:T(8,128)(2,1)}, bf16[2,16,16,640]{3,2,1,0:T(8,128)(2,1)}, bf16[2,16,16,192]{3,2,1,0:T(8,128...) custom-call(s32[1]{0:T(128)S(6)} %copy.15.counts_ref, s32[1,1024]{1,0:T(1,128)} %bitcast.4, ...), custom_call_target="tpu_custom_call" | custom-call | tf_op jit(solution)/shard_map/backward/pallas_call | solution.py:568
  109.9 3.4 %finish.1 = (bf16[1024,256]{1,0:T(8,128)(2,1)}, bf16[1024,256]{1,0:T(8,128)(2,1)}, f32[256,768]{1,0:T(8,128)}, f32[256,256]{1,0:T(8,128)}, f32[256,512]{1,0:T(8,128)}, /*index=5*/f32[512,256]{1,0:T(8,128)}) custom-call(bf16[1024,256]{1,0:T(8,128)(2,1)} %get-tuple-element.20.result_ref, bf16[1024,256]{1,0:T(8,128)(2,1)} %get-tuple-element.21.d_feats_ref, ...), custom_call_target="tpu_custom_call" | custom-call | tf_op jit(solution)/shard_map/finish/pallas_call | solution.py:679

commit v4 on v3

--- a/solution.py
+++ b/solution.py
@@ -16,6 +16,8 @@
 PAIR = 2
 STEPS = HEADS // PAIR
 HALF = 128
+BAND = 64
+BANDS = C1 // BAND
 SAFE_SCORE = 60.0
 MESH = pl.DeviceIdType.MESH
 BF = jnp.bfloat16
@@ -56,11 +58,19 @@
 
 def forward_kernel(
     counts_ref, feats_ref, gain_ref, w_qkv_ref,
-    raised_ref, proj_ref, scale_ref, att_ref,
-    keys_s, query_s, values_s, mixed_s, safe_s,
+    raised_hbm, proj_hbm, scale_ref, att_ref,
+    proj_ref, raised_s, keys_s, query_s, mixed_s, safe_s, store_sem, proj_sem,
 ):
     step = pl.program_id(0)
     live = counts_ref[0]
+    slot = lax.rem(step, 2)
+    store_proj = pltpu.make_async_copy(proj_ref, proj_hbm, proj_sem.at[0])
+
+    def store(at, one):
+        place = lax.rem(at, 2)
+        return pltpu.make_async_copy(
+            raised_s.at[place, one], raised_hbm.at[at * PAIR + one], store_sem.at[place, one]
+        )
 
     @pl.when(step == 0)
     def _():
@@ -68,53 +78,70 @@
         normed = (xhat * gain_ref[...]).astype(BF)
         proj = dg(w_qkv_ref[...], normed, 0, 1).astype(BF)
         proj_ref[...] = proj
+        store_proj.start()
         keys = dg(normed, w_qkv_ref[:, C1 : 2 * C1], 1, 0).astype(BF)
-        dead = (iota((ROWS, HALF), 0) >= live) & (iota((ROWS, HALF), 1) == 0)
+        dead = (iota((ROWS, BAND), 0) >= live) & (iota((ROWS, BAND), 1) == 0)
         bias = jnp.where(dead, -1e30, 0.0).astype(BF)
-        for half in range(2):
-            keys_s[half, :, :HALF] = keys[:, half * HALF : (half + 1) * HALF]
-            keys_s[half, :, HALF:] = bias
-        ones = jnp.where(iota((HALF, ROWS), 0) == 0, 1.0, 0.0).astype(BF)
+        for band in range(BANDS):
+            keys_s[band] = jnp.concatenate(
+                [keys[:, band * BAND : (band + 1) * BAND], bias], axis=1
+            )
+        ones = jnp.where(iota((BAND, ROWS), 0) == 0, 1.0, 0.0).astype(BF)
         for one in range(PAIR):
-            query_s[one, HALF:, :] = ones
-            values_s[one, HD:, :] = jnp.ones((HD, ROWS), BF)
+            query_s[one, BAND:, :] = ones
         wide = proj[: 2 * C1, :].astype(F32)
         squares = jnp.sum((wide * wide).reshape(2, HEADS, HD, ROWS), axis=2)
         bound = jnp.max(squares[0]) * jnp.max(squares[1]) / HD
         safe_s[0] = (bound <= SAFE_SCORE * SAFE_SCORE).astype(jnp.int32)
 
-    half = step // (STEPS // 2)
+    band = step // (STEPS // BANDS)
     for one in range(PAIR):
         head = step * PAIR + one
         start = pl.multiple_of(head * HD, HD)
-        place = pl.multiple_of(lax.rem(head, HEADS // 2) * HD, HD)
-        query_s[one, :HALF, :] = jnp.zeros((HALF, ROWS), BF)
+        place = pl.multiple_of(lax.rem(head, BAND // HD) * HD, HD)
+        query_s[one, :BAND, :] = jnp.zeros((BAND, ROWS), BF)
         query_s[one, pl.ds(place, HD), :] = proj_ref[pl.ds(start, HD), :] * jnp.asarray(
             HD ** (-0.5), BF
         )
-        values_s[one, :HD, :] = proj_ref[pl.ds(2 * C1 + start, HD), :]
+
+    @pl.when(step >= 2)
+    def _():
+        for one in range(PAIR):
+            store(step - 2, one).wait()
+
+    def attend(one, shifted):
+        scores = dg(keys_s[band], query_s[one], 1, 0)
+        if shifted:
+            scores = scores - jnp.max(scores, axis=0, keepdims=True)
+        raised = jnp.exp(scores)
+        scale = 1.0 / jnp.sum(raised, axis=0, keepdims=True)
+        raised_b = raised.astype(BF)
+        raised_s[slot, one] = raised_b
+        start = pl.multiple_of((step * PAIR + one) * HD, HD)
+        mixed_s[one] = dg(proj_ref[pl.ds(2 * C1 + start, HD), :], raised_b, 1, 0) * scale
+        scale_ref[one] = jnp.broadcast_to(scale, (8, ROWS))
+        store(step, one).start()
 
     @pl.when(safe_s[0] == 1)
     def _():
         for one in range(PAIR):
-            raised = jnp.exp(dg(keys_s[half], query_s[one], 1, 0)).astype(BF)
-            raised_ref[one] = raised
-            mixed_s[one] = dg(values_s[one], raised, 1, 0)
+            attend(one, False)
 
     @pl.when(safe_s[0] != 1)
     def _():
         for one in range(PAIR):
-            scores = dg(keys_s[half], query_s[one], 1, 0)
-            highest = jnp.max(scores, axis=0, keepdims=True)
-            raised = jnp.exp(scores - highest).astype(BF)
-            raised_ref[one] = raised
-            mixed_s[one] = dg(values_s[one], raised, 1, 0)
+            attend(one, True)
 
     for one in range(PAIR):
         start = pl.multiple_of((step * PAIR + one) * HD, HD)
-        scale = 1.0 / mixed_s[one, HD:, :]
-        att_ref[pl.ds(start, HD), :] = (mixed_s[one, :HD, :] * scale).astype(BF)
-        scale_ref[one] = scale[:8]
+        att_ref[pl.ds(start, HD), :] = mixed_s[one].astype(BF)
+
+    @pl.when(step == STEPS - 1)
+    def _():
+        store_proj.wait()
+        for one in range(PAIR):
+            store(step - 1, one).wait()
+            store(step, one).wait()
 
 
 def forward_call(counts, feats, gain, w_qkv):
@@ -129,8 +156,8 @@
             whole((C1, 3 * C1)),
         ],
         out_specs=[
-            per_pair(ROWS),
-            whole((3 * C1, ROWS)),
+            pl.BlockSpec(memory_space=pl.ANY),
+            pl.BlockSpec(memory_space=pl.ANY),
             per_pair(8),
             whole((C1, ROWS)),
         ],
@@ -141,11 +168,14 @@
             out((C1, ROWS), BF),
         ],
         scratch_shapes=[
-            pltpu.VMEM((2, ROWS, C1), BF),
-            pltpu.VMEM((PAIR, C1, ROWS), BF),
-            pltpu.VMEM((PAIR, 2 * HD, ROWS), BF),
-            pltpu.VMEM((PAIR, 2 * HD, ROWS), F32),
+            pltpu.VMEM((3 * C1, ROWS), BF),
+            pltpu.VMEM((2, PAIR, ROWS, ROWS), BF),
+            pltpu.VMEM((BANDS, ROWS, HALF), BF),
+            pltpu.VMEM((PAIR, HALF, ROWS), BF),
+            pltpu.VMEM((PAIR, HD, ROWS), F32),
             pltpu.SMEM((1,), jnp.int32),
+            pltpu.SemaphoreType.DMA((2, PAIR)),
+            pltpu.SemaphoreType.DMA((1,)),
         ],
         compiler_params=pltpu.CompilerParams(vmem_limit_bytes=56 * 2**20),
         name="forward",
@@ -171,14 +201,14 @@
 
 GROUP = 16
 UP_W = 2 * C1 + HALF
-EARLY_W = 2 * C1 + HALF
-EARLY_ROW, FIRST_ROW, SECOND_ROW, THIRD_ROW = 0, 5, 10, 15
-FIRST_HEADS, SECOND_HEADS, THIRD_HEADS = 8, 4, 4
-FIRST_W, SECOND_W, THIRD_W = (FIRST_HEADS * 24, SECOND_HEADS * 24, THIRD_HEADS * 48)
+EARLY_HEADS, LATE_HEADS, LAST_HEADS = 4, 10, 2
+GRADS_W = 2 * C1 + HALF
+EARLY_W = GRADS_W + EARLY_HEADS * 24
+LATE_W, LAST_W = LATE_HEADS * 24, LAST_HEADS * 48
+EARLY_ROW, LATE_ROW, LAST_ROW = 0, 5, 10
 SERVICES = (
-    (1, "early", 0), (5, "early", 1), (9, "early", 2), (13, "early", 3),
-    (8, "first", -1), (9, "first", 0), (13, "first", 1),
-    (12, "second", -1), (13, "second", 0),
+    (4, "early", -1), (5, "early", 0), (9, "early", 1), (13, "early", 2),
+    (14, "late", -1), (15, "late", 0),
 )
 
 
@@ -305,37 +335,57 @@
 
 
 def backward_kernel(
-    counts_ref, parent_ref, feats_ref, gain_ref, w_qkv_ref, w_out_ref, w_down_ref, w_up_ref,
-    cot_ref, att_ref, scale_ref, proj_hbm, raised_hbm,
-    result_ref, d_feats_ref, early_ref, first_ref, second_ref, third_ref,
-    proj_ref, raised_s, hidden_s, sum_s,
+    counts_ref, parent_ref, gain_ref,
+    att_hbm, feats_hbm, w_out_hbm, cot_hbm, w_qkv_hbm, w_down_hbm, w_up_hbm, proj_hbm, scale_hbm,
+    raised_hbm,
+    result_hbm, d_feats_hbm, early_hbm, late_hbm, last_hbm,
+    att_ref, feats_ref, w_out_ref, cot_ref, w_qkv_ref, w_down_ref, w_up_ref, proj_ref, scale_ref,
+    result_s, d_feats_s, raised_s, hidden_s, sum_s,
     d_hidden_s, normed_s, across_s, d_att_s, d_proj_s, values_s, cots_s, member_s, back_s,
     send_up, recv_up, send_down, recv_down,
     e_data, e_pair, e_half, e_got, e_line, e_full,
     f_data, f_pair, f_half, f_got, f_line, f_full,
-    s_data, s_pair, s_half, s_got, s_line, s_full,
     t_data, t_got, t_line, t_full,
-    near_send, near_recv, far_send, far_recv, load_sem,
+    near_send, near_recv, far_send, far_recv, load_sem, raised_sem, store_sem,
 ):
     step = pl.program_id(0)
     live = counts_ref[0]
     places = Places()
     sems = (far_send, far_recv)
     early = FiveStep(places, sems, EARLY_ROW, e_data, e_pair, e_half, e_got, e_line, e_full)
-    first = FiveStep(places, sems, FIRST_ROW, f_data, f_pair, f_half, f_got, f_line, f_full)
-    second = FiveStep(places, sems, SECOND_ROW, s_data, s_pair, s_half, s_got, s_line, s_full)
-    third = ThreeStep(places, sems, THIRD_ROW, t_data, t_got, t_line, t_full)
-    chunks = {"early": early, "first": first, "second": second, "third": third}
-    load_proj = pltpu.make_async_copy(proj_hbm, proj_ref, load_sem.at[2])
+    late = FiveStep(places, sems, LATE_ROW, f_data, f_pair, f_half, f_got, f_line, f_full)
+    last = ThreeStep(places, sems, LAST_ROW, t_data, t_got, t_line, t_full)
+    chunks = {"early": early, "late": late}
+    loads = [
+        pltpu.make_async_copy(src, dst, load_sem.at[n])
+        for n, (src, dst) in enumerate(
+            (
+                (att_hbm, att_ref), (feats_hbm, feats_ref), (w_out_hbm, w_out_ref),
+                (cot_hbm, cot_ref), (w_qkv_hbm, w_qkv_ref), (w_down_hbm, w_down_ref),
+                (w_up_hbm, w_up_ref), (proj_hbm, proj_ref), (scale_hbm, scale_ref),
+            )
+        )
+    ]
+    stores = [
+        pltpu.make_async_copy(src, dst, store_sem.at[n])
+        for n, (src, dst) in enumerate(
+            (
+                (result_s, result_hbm), (d_feats_s, d_feats_hbm), (e_full, early_hbm),
+                (f_full, late_hbm), (t_full, last_hbm),
+            )
+        )
+    ]
 
     def load_raised(at):
         slot = lax.rem(at, 2)
         return pltpu.make_async_copy(
-            raised_hbm.at[pl.ds(at * PAIR, PAIR)], raised_s.at[slot], load_sem.at[slot]
+            raised_hbm.at[pl.ds(at * PAIR, PAIR)], raised_s.at[slot], raised_sem.at[slot]
         )
 
     @pl.when(step == 0)
     def _():
+        for load in loads[:7]:
+            load.start()
         after, before = neighbour(1), neighbour(-1)
         barrier = pltpu.get_barrier_semaphore()
         for other in (after, before):
@@ -346,8 +396,11 @@
                 places.line_peer(lax.rem(places.line + k, GROUP)),
             ):
                 pl.semaphore_signal(barrier, inc=1, device_id=other, device_id_type=MESH)
-        load_proj.start()
+        for load in loads[7:]:
+            load.start()
         load_raised(0).start()
+        for load in loads[:4]:
+            load.wait()
 
         attended = att_ref[...].T
         hidden = (
@@ -379,17 +432,20 @@
         up.start()
         down.start()
 
+        for load in loads[4:7]:
+            load.wait()
         xhat, _ = norm_parts(feats_ref[...].astype(F32))
         normed = (xhat * gain_ref[...]).astype(BF)
         normed_s[...] = normed
         across_s[...] = normed.T
         values = dg(normed, w_qkv_ref[:, 2 * C1 :], 1, 0).astype(BF)
-        ones = jnp.where(iota((ROWS, HALF), 1) < 2, 1.0, 0.0).astype(BF)
-        for half in range(2):
-            values_s[half, :, :HALF] = values[:, half * HALF : (half + 1) * HALF]
-            values_s[half, :, HALF:] = ones
+        ones = jnp.where(iota((ROWS, BAND), 1) < 2, 1.0, 0.0).astype(BF)
+        for band in range(BANDS):
+            values_s[band] = jnp.concatenate(
+                [values[:, band * BAND : (band + 1) * BAND], ones], axis=1
+            )
         for one in range(PAIR):
-            cots_s[one] = jnp.zeros((C1, ROWS), BF)
+            cots_s[one] = jnp.zeros((HALF, ROWS), BF)
         column = jnp.broadcast_to(local.astype(F32), (HALF, ROWS)).T[:, :1].astype(jnp.int32)
         member = (column == iota((ROWS, TABLE), 1)) & (iota((ROWS, TABLE), 0) < live)
         member_s[...] = jnp.where(member, 1.0, 0.0).astype(BF)
@@ -434,9 +490,10 @@
         share_high = share.astype(BF)
         share_low = (share - share_high.astype(F32)).astype(BF)
         grad_up = dg(activ[:CORE], d_back[:CORE], 0, 0).astype(BF)
-        e_data[:, :, :, :C1] = grad_up.reshape(2, GROUP, 16, C1)
+        grad_up = grad_up.reshape(GROUP, 2, 16, C1)
         grad_down = dg(pooled[:CORE], d_pre[:CORE], 0, 0).astype(BF).reshape(GROUP, 16, C2)
         for core in range(2):
+            e_data[core, :, :, :C1] = grad_up[:, core]
             e_data[core, :, :, C1 : 2 * C1] = grad_down[:, :, core * C1 : (core + 1) * C1]
         member_b = member_s[...]
         d_hidden = (
@@ -448,10 +505,10 @@
         d_hidden_b = d_hidden.astype(BF)
         grad_out = dg(att_ref[...], d_hidden_b, 1, 0).astype(BF).reshape(GROUP, 16, C1)
         for core in range(2):
-            e_data[core, :, :, 2 * C1 :] = grad_out[:, :, core * HALF : (core + 1) * HALF]
-        early.begin()
+            e_data[core, :, :, 2 * C1 : GRADS_W] = grad_out[:, :, core * HALF : (core + 1) * HALF]
         d_att_s[...] = dg(w_out_ref[...], d_hidden_b, 1, 1).astype(BF)
-        load_proj.wait()
+        for load in loads[7:]:
+            load.wait()
 
     @pl.when(step < STEPS - 1)
     def _():
@@ -466,23 +523,25 @@
         ]
         return dg(across_s[...], jnp.concatenate(rows, axis=0), 1, 1).astype(BF)
 
-    def fill_halves(data, head, heads):
+    def fill_halves(data, first, head, heads):
         grads = grad_columns(head, heads)
         width = 3 * heads * HD // 2
         for core in range(2):
-            data[core] = grads[:, core * width : (core + 1) * width].reshape(GROUP, 16, width)
+            data[core, :, :, first : first + width] = grads[
+                :, core * width : (core + 1) * width
+            ].reshape(GROUP, 16, width)
 
     def serve(name, stage):
         if stage >= 0:
             chunks[name].advance(stage)
             return
-        if name == "first":
-            fill_halves(f_data, 0, FIRST_HEADS)
+        if name == "early":
+            fill_halves(e_data, GRADS_W, 0, EARLY_HEADS)
         else:
-            fill_halves(s_data, FIRST_HEADS, SECOND_HEADS)
+            fill_halves(f_data, 0, EARLY_HEADS, LATE_HEADS)
         chunks[name].begin()
 
-    half = step // (STEPS // 2)
+    band = step // (STEPS // BANDS)
     quarter = jnp.asarray(HD ** (-0.5), BF)
     for one in range(PAIR):
         for turn, name, stage in SERVICES:
@@ -493,20 +552,20 @@
 
         head = step * PAIR + one
         start = pl.multiple_of(head * HD, HD)
-        place = pl.multiple_of(lax.rem(head, HEADS // 2) * HD, HD)
-        cot = (d_att_s[pl.ds(start, HD), :].astype(F32) * scale_ref[one, :1, :]).astype(BF)
+        place = pl.multiple_of(lax.rem(head, BAND // HD) * HD, HD)
+        cot = (d_att_s[pl.ds(start, HD), :].astype(F32) * scale_ref[head, :1, :]).astype(BF)
         inner = -jnp.sum(
             cot.astype(F32) * att_ref[pl.ds(start, HD), :].astype(F32), axis=0, keepdims=True
         )
         high = inner.astype(BF).astype(F32)
         rows = iota((HD, ROWS), 0)
-        cots_s[one, :HALF, :] = jnp.zeros((HALF, ROWS), BF)
+        cots_s[one, :BAND, :] = jnp.zeros((BAND, ROWS), BF)
         cots_s[one, pl.ds(place, HD), :] = cot
-        cots_s[one, HALF : HALF + HD, :] = jnp.where(
+        cots_s[one, BAND : BAND + HD, :] = jnp.where(
             rows == 0, high, jnp.where(rows == 1, inner - high, 0.0)
         ).astype(BF)
         raised = raised_s[lax.rem(step, 2), one]
-        d_scores = raised * dg(values_s[half], cots_s[one], 1, 0).astype(BF)
+        d_scores = raised * dg(values_s[band], cots_s[one], 1, 0).astype(BF)
         d_proj_s[pl.ds(start, HD), :] = dg(
             proj_ref[pl.ds(C1 + start, HD), :] * quarter, d_scores, 1, 0
         ).astype(BF)
@@ -517,47 +576,47 @@
 
     @pl.when(step == STEPS - 1)
     def _():
-        grads = grad_columns(FIRST_HEADS + SECOND_HEADS, THIRD_HEADS)
-        t_data[...] = grads.reshape(GROUP, 16, THIRD_W)
-        third.begin()
-        early.advance(4)
-        first.advance(2)
+        grads = grad_columns(EARLY_HEADS + LATE_HEADS, LAST_HEADS)
+        t_data[...] = grads.reshape(GROUP, 16, LAST_W)
+        last.begin()
         d_normed = dg(w_qkv_ref[...], d_proj_s[...], 1, 0).T
-        second.advance(1)
+        early.advance(3)
+        late.advance(1)
         xhat, inverse = norm_parts(feats_ref[...].astype(F32))
         grown = d_normed * gain_ref[...]
         along = jnp.mean(grown * xhat, axis=-1, keepdims=True)
         d_wide = inverse * (grown - jnp.mean(grown, axis=-1, keepdims=True) - xhat * along)
-        d_feats_ref[...] = (d_hidden_s[...] + d_wide).astype(BF)
-        third.advance(0)
-        first.advance(3)
-        result_ref[...] = (
+        d_feats_s[...] = (d_hidden_s[...] + d_wide).astype(BF)
+        stores[1].start()
+        last.advance(0)
+        early.advance(4)
+        stores[2].start()
+        result_s[...] = (
             hidden_s[...].astype(F32) + dg(member_s[...], back_s[...], 1, 0)
         ).astype(BF)
-        early_ref[...] = e_full[...]
-        second.advance(2)
-        third.advance(1)
-        first.advance(4)
-        first_ref[...] = f_full[...]
-        second.advance(3)
-        second.advance(4)
-        second_ref[...] = s_full[...]
-        third.advance(2)
-        third_ref[...] = t_full[...]
-
-
-def backward_call(
-    counts, parent, feats, gain, w_qkv, w_out, w_down, w_up, cotangent,
-    att, scale, proj, raised,
-):
+        stores[0].start()
+        late.advance(2)
+        last.advance(1)
+        late.advance(3)
+        late.advance(4)
+        stores[3].start()
+        last.advance(2)
+        stores[4].start()
+        for store in stores:
+            store.wait()
+
+
+def backward_call(counts, parent, gain, att, feats, w_out, cotangent, w_qkv, w_down, w_up,
+                  proj, scale, raised):
     out = jax.ShapeDtypeStruct
     vmem = pltpu.VMEM
-    early, first, second, third = (
+    anywhere = pl.BlockSpec(memory_space=pl.ANY)
+    early, late, last = (
         (2, GROUP, 16, EARLY_W),
-        (2, GROUP, 16, FIRST_W),
-        (2, GROUP, 16, SECOND_W),
-        (GROUP, 16, THIRD_W),
+        (2, GROUP, 16, LATE_W),
+        (GROUP, 16, LAST_W),
     )
+    loaded = (att, feats, w_out, cotangent, w_qkv, w_down, w_up, proj, scale)
 
     def five(shape):
         return [
@@ -571,36 +630,21 @@
         in_specs=[
             pl.BlockSpec(memory_space=pltpu.SMEM),
             whole((1, ROWS)),
-            whole((ROWS, C1)),
             whole((1, C1)),
-            whole((C1, 3 * C1)),
-            whole((C1, C1)),
-            whole((C1, C2)),
-            whole((C2, C1)),
-            whole((ROWS, C1)),
-            whole((C1, ROWS)),
-            per_pair(8),
-            pl.BlockSpec(memory_space=pl.ANY),
-            pl.BlockSpec(memory_space=pl.ANY),
-        ],
-        out_specs=[
-            whole((ROWS, C1)),
-            whole((ROWS, C1)),
-            whole(early),
-            whole(first),
-            whole(second),
-            whole(third),
-        ],
+        ]
+        + [anywhere] * 10,
+        out_specs=[anywhere] * 5,
         out_shape=[
             out((ROWS, C1), BF),
             out((ROWS, C1), BF),
             out(early, BF),
-            out(first, BF),
-            out(second, BF),
-            out(third, BF),
+            out(late, BF),
+            out(last, BF),
         ],
-        scratch_shapes=[
-            vmem((3 * C1, ROWS), BF),
+        scratch_shapes=[vmem(array.shape, array.dtype) for array in loaded]
+        + [
+            vmem((ROWS, C1), BF),
+            vmem((ROWS, C1), BF),
             vmem((2, PAIR, ROWS, ROWS), BF),
             vmem((ROWS, C1), BF),
             vmem((TABLE, UP_W), F32),
@@ -609,8 +653,8 @@
             vmem((C1, ROWS), BF),
             vmem((C1, ROWS), BF),
             vmem((3 * C1, ROWS), BF),
-            vmem((2, ROWS, C1), BF),
-            vmem((PAIR, C1, ROWS), BF),
+            vmem((BANDS, ROWS, HALF), BF),
+            vmem((PAIR, HALF, ROWS), BF),
             vmem((ROWS, TABLE), BF),
             vmem((TABLE, C1), BF),
             vmem((SPILL, UP_W), BF),
@@ -619,69 +663,105 @@
             vmem((SPILL, UP_W), BF),
         ]
         + five(early)
-        + five(first)
-        + five(second)
-        + [vmem(third, BF)] * 4
+        + five(late)
+        + [vmem(last, BF)] * 4
         + [
             pltpu.SemaphoreType.DMA((2,)),
             pltpu.SemaphoreType.DMA((2,)),
-            pltpu.SemaphoreType.DMA((18,)),
-            pltpu.SemaphoreType.DMA((18,)),
-            pltpu.SemaphoreType.DMA((3,)),
+            pltpu.SemaphoreType.DMA((13,)),
+            pltpu.SemaphoreType.DMA((13,)),
+            pltpu.SemaphoreType.DMA((9,)),
+            pltpu.SemaphoreType.DMA((2,)),
+            pltpu.SemaphoreType.DMA((5,)),
         ],
         compiler_params=pltpu.CompilerParams(
             collective_id=0, has_side_effects=True, vmem_limit_bytes=58 * 2**20
         ),
         name="backward",
-    )(
-        counts, parent, feats, gain, w_qkv, w_out, w_down, w_up, cotangent,
-        att, scale, proj, raised,
-    )
+    )(counts, parent, gain, *loaded, raised)
 
 
 def finish_kernel(
-    result_ref, d_feats_ref, early_ref, first_ref, second_ref, third_ref,
+    result_hbm, d_feats_hbm, early_hbm, late_hbm, last_hbm,
     result_out, d_feats_out, qkv_out, out_out, down_out, up_out,
+    result_s, d_feats_s, early_ref, late_ref, last_ref, qkv_s, out_s, down_s, up_s, load_sem, pass_sem, store_sem,
 ):
-    result_out[...] = result_ref[...]
-    d_feats_out[...] = d_feats_ref[...]
+    loads = [
+        pltpu.make_async_copy(src, dst, load_sem.at[n])
+        for n, (src, dst) in enumerate(
+            (
+                (early_hbm, early_ref), (late_hbm, late_ref), (last_hbm, last_ref),
+                (result_hbm, result_s), (d_feats_hbm, d_feats_s),
+            )
+        )
+    ]
+    passes = [
+        pltpu.make_async_copy(result_s, result_out, pass_sem.at[0]),
+        pltpu.make_async_copy(d_feats_s, d_feats_out, pass_sem.at[1]),
+    ]
+    stores = [
+        pltpu.make_async_copy(src, dst, store_sem.at[n])
+        for n, (src, dst) in enumerate(
+            ((qkv_s, qkv_out), (out_s, out_out), (down_s, down_out), (up_s, up_out))
+        )
+    ]
+    for load in loads:
+        load.start()
+    loads[0].wait()
     for core in range(2):
-        piece = early_ref[core]
-        up_out[core * C1 : (core + 1) * C1, :] = piece[:, :, :C1].reshape(C1, C1).astype(F32)
-        down_out[:, core * C1 : (core + 1) * C1] = (
-            piece[:, :, C1 : 2 * C1].reshape(C1, C1).astype(F32)
-        )
-        out_out[:, core * HALF : (core + 1) * HALF] = (
-            piece[:, :, 2 * C1 :].reshape(C1, HALF).astype(F32)
-        )
-    low, high = [
-        jnp.concatenate([ref[core].reshape(C1, width).astype(F32) for core in range(2)], axis=1)
-        for ref, width in ((first_ref, FIRST_W), (second_ref, SECOND_W))
+        up_s[:, core] = early_ref[core, :, :, :C1].astype(F32)
+        down_s[:, core * C1 : (core + 1) * C1] = (
+            early_ref[core, :, :, C1 : 2 * C1].reshape(C1, C1).astype(F32)
+        )
+        out_s[:, core * HALF : (core + 1) * HALF] = (
+            early_ref[core, :, :, 2 * C1 : GRADS_W].reshape(C1, HALF).astype(F32)
+        )
+    for store in stores[1:]:
+        store.start()
+    for load in loads[1:]:
+        load.wait()
+    for one in passes:
+        one.start()
+    early, late = [
+        jnp.concatenate(
+            [ref[core, :, :, first:].astype(F32).reshape(C1, -1) for core in range(2)], axis=1
+        )
+        for ref, first in ((early_ref, GRADS_W), (late_ref, 0))
     ]
-    last = third_ref[...].reshape(C1, THIRD_W).astype(F32)
+    last = last_ref[...].astype(F32).reshape(C1, LAST_W)
     for part in range(3):
-        qkv_out[:, part * C1 : (part + 1) * C1] = jnp.concatenate(
+        qkv_s[:, part * C1 : (part + 1) * C1] = jnp.concatenate(
             [
                 piece[:, part * heads * HD : (part + 1) * heads * HD]
                 for piece, heads in (
-                    (low, FIRST_HEADS), (high, SECOND_HEADS), (last, THIRD_HEADS)
+                    (early, EARLY_HEADS), (late, LATE_HEADS), (last, LAST_HEADS)
                 )
             ],
             axis=1,
         )
+    stores[0].start()
+    for copy in passes + stores:
+        copy.wait()
 
 
 def finish_call(*parts):
+    anywhere = pl.BlockSpec(memory_space=pl.ANY)
     shapes = [
         ((ROWS, C1), BF), ((ROWS, C1), BF), ((C1, 3 * C1), F32), ((C1, C1), F32),
-        ((C1, C2), F32), ((C2, C1), F32),
+        ((C1, C2), F32), ((GROUP, 2, 16, C1), F32),
     ]
     return pl.pallas_call(
         finish_kernel,
-        grid=(1,),
-        in_specs=[whole(part.shape) for part in parts],
-        out_specs=[whole(shape) for shape, _ in shapes],
+        in_specs=[anywhere] * 5,
+        out_specs=[anywhere] * 6,
         out_shape=[jax.ShapeDtypeStruct(shape, kind) for shape, kind in shapes],
+        scratch_shapes=[pltpu.VMEM(part.shape, BF) for part in parts]
+        + [pltpu.VMEM(shape, F32) for shape, _ in shapes[2:]]
+        + [
+            pltpu.SemaphoreType.DMA((5,)),
+            pltpu.SemaphoreType.DMA((2,)),
+            pltpu.SemaphoreType.DMA((4,)),
+        ],
         compiler_params=pltpu.CompilerParams(vmem_limit_bytes=60 * 2**20),
         name="finish",
     )(*parts)
@@ -692,10 +772,11 @@
     gain = ln_gain.reshape(1, C1)
     raised, proj, scale, att = forward_call(counts, feats, gain, w_qkv)
     parts = backward_call(
-        counts, parent_row, feats, gain, w_qkv, w_out, w_down, w_up, cotangent,
-        att, scale, proj, raised,
+        counts, parent_row, gain, att, feats, w_out, cotangent, w_qkv, w_down, w_up,
+        proj, scale, raised,
     )
-    return tuple(finish_call(*parts))
+    result, d_feats, grad_qkv, grad_out, grad_down, grad_up = finish_call(*parts)
+    return (result, d_feats, grad_qkv, grad_out, grad_down, grad_up.reshape(C2, C1))
 
 
 def solution(mesh):

time: 113 us -> 108 us (0.956)
  Pallas kernels: 112 us -> 106 us
    pallas_call x1, Pallas kernels: 73.3 us -> 70.2 us  [backward_call(): pl.pallas_call(backward_kernel, grid=(STEPS,), in_specs=[pl.BlockSpec(mem...]
    pallas_call x1, Pallas kernels: 35.3 us -> 33.1 us  [forward_call(): pl.pallas_call(forward_kernel, grid=(STEPS,), in_specs=[pl.BlockSpec(memo...]
where the time goes in v4:
time: 108 us
  Pallas kernels  106 us (98%)
  between operations  1.45 us (1%)
    pallas_call x1, Pallas kernels, backward_call(): pl.pallas_call(backward_kernel, grid=(STEPS,), in_specs=[pl.BlockSpec(mem...  70.2 us
    pallas_call x1, Pallas kernels, forward_call(): pl.pallas_call(forward_kernel, grid=(STEPS,), in_specs=[pl.BlockSpec(memo...  33.1 us
    pallas_call x1, Pallas kernels, finish_call(): pl.pallas_call(finish_kernel, in_specs=[anywhere] * 5, out_specs=[anywher...  2.91 us

profile of v4, /device:TPU:1, one launch (start us, length us, event | category | flops | bytes accessed | tf_op | source)
XLA Modules:
  0.0 107.7 jit_solution(88838769700125774)
XLA Ops:
  1.3 33.1 %forward.1 = (bf16[16,1024,1024]{2,1,0:T(8,128)(2,1)}, bf16[768,1024]{1,0:T(8,128)(2,1)}, f32[16,8,1024]{2,1,0:T(8,128)}, bf16[256,1024]{1,0:T(8,128)(2,1)}) custom-call(s32[1]{0:T(128)S(6)} %copy.15.counts_ref, bf16[1024,256]{1,0:T(8,128)(2,1)} %feats_hbm.1, f32[1,256]{1,0:T(1,128)} %bitcast.3, bf16[256,768]{1,0:T(8,128)(2,1)} %w_qkv_hbm.1), custom_call_target="tpu_custom_call" | custom-call | tf_op jit(solution)/shard_map/forward/pallas_call | solution.py:149
  34.4 70.2 %backward.1 = (bf16[1024,256]{1,0:T(8,128)(2,1)}, bf16[1024,256]{1,0:T(8,128)(2,1)}, bf16[2,16,16,736]{3,2,1,0:T(8,128)(2,1)}, bf16[2,16,16,240]{3,2,1,0:T(8,128)(2,1)}, bf16[16,16,96]{2,1,0:T(8,128)(2,1)}) custom-call(s32[1]{0:T(128)S(6)} %copy.15.counts_ref, s32[1,1024]{1,0:T(1,128)} %bitcast.5, f32[1,256]{1,0:T(1,128)} %bitcast.4, ...), custom_call_target="tpu_custom_call" | custom-call | tf_op jit(solution)/shard_map/backward/pallas_call | solution.py:627
  104.6 2.9 %finish.1 = (bf16[1024,256]{1,0:T(8,128)(2,1)}, bf16[1024,256]{1,0:T(8,128)(2,1)}, f32[256,768]{1,0:T(8,128)}, f32[256,256]{1,0:T(8,128)}, f32[256,512]{1,0:T(8,128)}, /*index=5*/f32[16,2,16,256]{3,2,1,0:T(8,128)}) custom-call(bf16[1024,256]{1,0:T(8,128)(2,1)} %get-tuple-element.25.result_hbm, bf16[1024,256]{1,0:T(8,128)(2,1)} %get-tuple-element.26.d_feats_hbm, ...), custom_call_target="tpu_custom_call" | custom-call | tf_op jit(solution)/shard_map/finish/pallas_call | solution.py:753

commit v5 on v4

--- a/solution.py
+++ b/solution.py
@@ -13,6 +13,7 @@
 CORE = 256
 SPILL = 64
 TABLE = CORE + SPILL
+EDGE = 2 * SPILL
 PAIR = 2
 STEPS = HEADS // PAIR
 HALF = 128
@@ -212,6 +213,14 @@
 )
 
 
+FAR_FIRST = {
+    2: (1,),
+    8: (4, 3, 5, 2, 6, 1, 7),
+    "plane": (10, 9, 11, 6, 14, 8, 2, 5, 7, 13, 15, 1, 3, 4, 12),
+    "line": (8, 9, 7, 6, 10, 5, 11, 4, 12, 3, 13, 2, 14, 1, 15),
+}
+
+
 class Places:
     def __init__(self):
         pts, self.y = lax.axis_index("pts"), lax.axis_index("grp")
@@ -235,7 +244,8 @@
 
 
 class Exchange:
-    def __init__(self, sems, row, members, me, peer, src, slots):
+    def __init__(self, places, sems, row, members, me, peer, src, slots):
+        self.places = places
         self.send, self.recv = sems
         self.row, self.members, self.me, self.peer = row, members, me, peer
         self.src, self.slots = src, slots
@@ -251,15 +261,23 @@
         )
 
     def start(self):
-        for k in range(1, self.members):
+        if self.members == GROUP:
+            order = FAR_FIRST["line" if self.peer == self.places.line_peer else "plane"]
+        else:
+            order = FAR_FIRST[self.members]
+        for k in order:
             src = self.src(lax.rem(self.me + k, self.members))
             self.copy(src, self.slots.at[self.me], k).start()
 
+    def whole(self):
+        others = self.slots.at[pl.ds(0, self.members - 1)]
+        return self.copy(others, others, 1)
+
     def wait(self):
-        others = self.slots.at[pl.ds(0, self.members - 1)]
-        copy = self.copy(others, others, 1)
-        copy.wait_send()
-        copy.wait_recv()
+        self.whole().wait_recv()
+
+    def drain(self):
+        self.whole().wait_send()
 
 
 def add_slots(ref):
@@ -272,15 +290,15 @@
         self.places, self.data, self.pair, self.half = places, data, pair, half
         self.got, self.line, self.full = got, line, full
         self.stages = [
-            Exchange(sems, row, 2, core, places.core_peer,
+            Exchange(places, sems, row, 2, core, places.core_peer,
                      lambda j: data.at[j], pair),
-            Exchange(sems, row + 1, GROUP, plane, places.plane_peer,
+            Exchange(places, sems, row + 1, GROUP, plane, places.plane_peer,
                      lambda j: half.at[j], got),
-            Exchange(sems, row + 2, 8, places.z, places.column_peer,
+            Exchange(places, sems, row + 2, 8, places.z, places.column_peer,
                      lambda j: line.at[places.z], line),
-            Exchange(sems, row + 3, GROUP, plane, places.plane_peer,
+            Exchange(places, sems, row + 3, GROUP, plane, places.plane_peer,
                      lambda j: full.at[core, plane], full.at[core]),
-            Exchange(sems, row + 4, 2, core, places.core_peer,
+            Exchange(places, sems, row + 4, 2, core, places.core_peer,
                      lambda j: full.at[core], full),
         ]
 
@@ -310,11 +328,11 @@
         self.places, self.data, self.got = places, data, got
         self.line, self.full = line, full
         self.stages = [
-            Exchange(sems, row, GROUP, plane, places.plane_peer,
+            Exchange(places, sems, row, GROUP, plane, places.plane_peer,
                      lambda j: data.at[j], got),
-            Exchange(sems, row + 1, GROUP, places.line, places.line_peer,
+            Exchange(places, sems, row + 1, GROUP, places.line, places.line_peer,
                      lambda j: line.at[places.line], line),
-            Exchange(sems, row + 2, GROUP, plane, places.plane_peer,
+            Exchange(places, sems, row + 2, GROUP, plane, places.plane_peer,
                      lambda j: full.at[plane], full),
         ]
 
@@ -376,6 +394,16 @@
         )
     ]
 
+    after, before = neighbour(1), neighbour(-1)
+    near = [
+        pltpu.make_async_remote_copy(
+            src, dst, near_send.at[n], near_recv.at[n], device_id=other, device_id_type=MESH
+        )
+        for n, (src, dst, other) in enumerate(
+            ((send_up, recv_up, after), (send_down, recv_down, before))
+        )
+    ]
+
     def load_raised(at):
         slot = lax.rem(at, 2)
         return pltpu.make_async_copy(
@@ -384,18 +412,19 @@
 
     @pl.when(step == 0)
     def _():
-        for load in loads[:7]:
-            load.start()
-        after, before = neighbour(1), neighbour(-1)
         barrier = pltpu.get_barrier_semaphore()
         for other in (after, before):
             pl.semaphore_signal(barrier, inc=1, device_id=other, device_id_type=MESH)
-        for k in range(1, GROUP):
+        for load in loads[:4]:
+            load.start()
+        for in_plane, in_line in zip(FAR_FIRST["plane"], FAR_FIRST["line"]):
             for other in (
-                places.plane_peer(lax.rem(places.plane + k, GROUP)),
-                places.line_peer(lax.rem(places.line + k, GROUP)),
+                places.plane_peer(lax.rem(places.plane + in_plane, GROUP)),
+                places.line_peer(lax.rem(places.line + in_line, GROUP)),
             ):
                 pl.semaphore_signal(barrier, inc=1, device_id=other, device_id_type=MESH)
+        for load in loads[4:7]:
+            load.start()
         for load in loads[7:]:
             load.start()
         load_raised(0).start()
@@ -408,29 +437,26 @@
         ).astype(BF)
         hidden_s[...] = hidden
         local = parent_ref[...] - device_number() * CORE
+        local = jnp.where(
+            local < SPILL,
+            local,
+            jnp.where(local < CORE, local + SPILL, local - (CORE - SPILL)),
+        )
         member = (local == iota((TABLE, ROWS), 0)) & (iota((TABLE, ROWS), 1) < live)
         member_f = jnp.where(member, 1.0, 0.0)
         counted = jnp.sum(member_f, axis=1, keepdims=True)
         sum_s[:, :C1] = dg(member_f.astype(BF), hidden, 1, 0)
         sum_s[:, C1 : 2 * C1] = dg(member_f.astype(BF), cot_ref[...], 1, 0)
         sum_s[:, 2 * C1 :] = jnp.broadcast_to(counted, (TABLE, HALF))
-        for buf, rows in ((send_up, slice(CORE, TABLE)), (send_down, slice(0, SPILL))):
+        for buf, rows in ((send_up, slice(SPILL, EDGE)), (send_down, slice(0, SPILL))):
             buf[:, : 2 * C1] = sum_s[rows, : 2 * C1].astype(BF)
             count = sum_s[rows, 2 * C1 :]
             high = count.astype(BF)
             low = (count - high.astype(F32)).astype(BF)
             buf[:, 2 * C1 :] = jnp.where(iota((SPILL, HALF), 1) < HALF // 2, high, low)
         pl.semaphore_wait(barrier, 2 * GROUP)
-        up = pltpu.make_async_remote_copy(
-            send_up, recv_up, near_send.at[0], near_recv.at[0],
-            device_id=after, device_id_type=MESH,
-        )
-        down = pltpu.make_async_remote_copy(
-            send_down, recv_down, near_send.at[1], near_recv.at[1],
-            device_id=before, device_id_type=MESH,
-        )
-        up.start()
-        down.start()
+        for copy in near:
+            copy.start()
 
         for load in loads[4:7]:
             load.wait()
@@ -450,63 +476,69 @@
         member = (column == iota((ROWS, TABLE), 1)) & (iota((ROWS, TABLE), 0) < live)
         member_s[...] = jnp.where(member, 1.0, 0.0).astype(BF)
 
-        up.wait()
-        down.wait()
-        sums = []
-        for buf, rows in ((recv_up, slice(0, SPILL)), (recv_down, slice(CORE, TABLE))):
-            got = buf[...].astype(F32)
-            count_in = (
-                got[:, 2 * C1 : 2 * C1 + 1]
-                + got[:, 2 * C1 + HALF // 2 : 2 * C1 + HALF // 2 + 1]
+        def coarse(total, total_cot, counted):
+            inverse = 1.0 / jnp.maximum(counted, 1.0)
+            pooled = (total * inverse).astype(BF)
+            value, slope = gelu_and_slope(dg(pooled, w_down_ref[...], 1, 0))
+            activ = value.astype(BF)
+            back = dg(activ, w_up_ref[...], 1, 0).astype(BF)
+            d_back = total_cot.astype(BF)
+            d_pre = (dg(d_back, w_up_ref[...], 1, 1) * slope).astype(BF)
+            share = dg(d_pre, w_down_ref[...], 1, 1) * inverse
+            high = share.astype(BF)
+            low = (share - high.astype(F32)).astype(BF)
+            return pooled, activ, back, d_back, d_pre, high, low
+
+        middle = slice(EDGE, TABLE)
+        pooled, activ, back, d_back, d_pre, high, low = coarse(
+            sum_s[middle, :C1],
+            sum_s[middle, C1 : 2 * C1],
+            sum_s[middle, 2 * C1 : 2 * C1 + 1],
+        )
+        back_s[middle, :] = back
+        grad_up = dg(activ, d_back, 0, 0)
+        grad_down = dg(pooled, d_pre, 0, 0)
+        inner = member_s[:, middle]
+        d_hidden_s[...] = (
+            cot_ref[...].astype(F32) + dg(inner, high, 1, 0) + dg(inner, low, 1, 0)
+        )
+
+        for copy in near:
+            copy.wait_recv()
+        got = jnp.concatenate([recv_up[...], recv_down[...]], axis=0).astype(F32)
+        count_in = (
+            got[:, 2 * C1 : 2 * C1 + 1]
+            + got[:, 2 * C1 + HALF // 2 : 2 * C1 + HALF // 2 + 1]
+        )
+        pooled, activ, back, d_back, d_pre, high, low = coarse(
+            sum_s[:EDGE, :C1] + got[:, :C1],
+            sum_s[:EDGE, C1 : 2 * C1] + got[:, C1 : 2 * C1],
+            sum_s[:EDGE, 2 * C1 : 2 * C1 + 1] + count_in,
+        )
+        outer = member_s[:, :EDGE]
+        d_hidden = (
+            d_hidden_s[...]
+            + dg(
+                jnp.concatenate([outer, outer], axis=1),
+                jnp.concatenate([high, low], axis=0),
+                1,
+                0,
             )
-            sums.append(
-                (
-                    sum_s[rows, :C1] + got[:, :C1],
-                    sum_s[rows, C1 : 2 * C1] + got[:, C1 : 2 * C1],
-                    sum_s[rows, 2 * C1 : 2 * C1 + 1] + count_in,
-                )
-            )
-        middle = slice(SPILL, CORE)
-        sums.insert(
-            1,
-            (
-                sum_s[middle, :C1],
-                sum_s[middle, C1 : 2 * C1],
-                sum_s[middle, 2 * C1 : 2 * C1 + 1],
-            ),
-        )
-        own_sum, own_cot, counted = [
-            jnp.concatenate([piece[n] for piece in sums], axis=0) for n in range(3)
-        ]
-        inverse = 1.0 / jnp.maximum(counted, 1.0)
-        pooled = (own_sum * inverse).astype(BF)
-        pre = dg(pooled, w_down_ref[...], 1, 0)
-        value, slope = gelu_and_slope(pre)
-        activ = value.astype(BF)
-        back_s[...] = dg(activ, w_up_ref[...], 1, 0).astype(BF)
-        d_back = own_cot.astype(BF)
-        d_pre = (dg(d_back, w_up_ref[...], 1, 1) * slope).astype(BF)
-        share = dg(d_pre, w_down_ref[...], 1, 1) * inverse
-        share_high = share.astype(BF)
-        share_low = (share - share_high.astype(F32)).astype(BF)
-        grad_up = dg(activ[:CORE], d_back[:CORE], 0, 0).astype(BF)
+        )
+        d_hidden_s[...] = d_hidden
+        d_hidden_b = d_hidden.astype(BF)
+        d_att_s[...] = dg(w_out_ref[...], d_hidden_b, 1, 1).astype(BF)
+        back_s[:EDGE, :] = back
+        grad_up = (grad_up + dg(activ[:SPILL], d_back[:SPILL], 0, 0)).astype(BF)
         grad_up = grad_up.reshape(GROUP, 2, 16, C1)
-        grad_down = dg(pooled[:CORE], d_pre[:CORE], 0, 0).astype(BF).reshape(GROUP, 16, C2)
+        grad_down = (grad_down + dg(pooled[:SPILL], d_pre[:SPILL], 0, 0)).astype(BF)
+        grad_down = grad_down.reshape(GROUP, 16, C2)
         for core in range(2):
             e_data[core, :, :, :C1] = grad_up[:, core]
             e_data[core, :, :, C1 : 2 * C1] = grad_down[:, :, core * C1 : (core + 1) * C1]
-        member_b = member_s[...]
-        d_hidden = (
-            cot_ref[...].astype(F32)
-            + dg(member_b, share_high, 1, 0)
-            + dg(member_b, share_low, 1, 0)
-        )
-        d_hidden_s[...] = d_hidden
-        d_hidden_b = d_hidden.astype(BF)
         grad_out = dg(att_ref[...], d_hidden_b, 1, 0).astype(BF).reshape(GROUP, 16, C1)
         for core in range(2):
             e_data[core, :, :, 2 * C1 : GRADS_W] = grad_out[:, :, core * HALF : (core + 1) * HALF]
-        d_att_s[...] = dg(w_out_ref[...], d_hidden_b, 1, 1).astype(BF)
         for load in loads[7:]:
             load.wait()
 
@@ -602,6 +634,11 @@
         stores[3].start()
         last.advance(2)
         stores[4].start()
+        for chunk in (early, late, last):
+            for stage in chunk.stages:
+                stage.drain()
+        for copy in near:
+            copy.wait_send()
         for store in stores:
             store.wait()
 

time: 108 us -> 106 us (0.981)
    pallas_call x1, Pallas kernels: 70.2 us -> 68.5 us  [backward_call(): pl.pallas_call(backward_kernel, grid=(STEPS,), in_specs=[pl.BlockSpec(mem...]
where the time goes in v5:
time: 106 us
  Pallas kernels  105 us (99%)
  between operations  1.45 us (1%)
    pallas_call x1, Pallas kernels, backward_call(): pl.pallas_call(backward_kernel, grid=(STEPS,), in_specs=[pl.BlockSpec(mem...  68.5 us
    pallas_call x1, Pallas kernels, forward_call(): pl.pallas_call(forward_kernel, grid=(STEPS,), in_specs=[pl.BlockSpec(memo...  33.1 us
    pallas_call x1, Pallas kernels, finish_call(): pl.pallas_call(finish_kernel, in_specs=[anywhere] * 5, out_specs=[anywher...  2.91 us

profile of v5, /device:TPU:1, one launch (start us, length us, event | category | flops | bytes accessed | tf_op | source)
XLA Modules:
  0.0 106.0 jit_solution(17708120708106330102)
XLA Ops:
  1.3 33.1 %forward.1 = (bf16[16,1024,1024]{2,1,0:T(8,128)(2,1)}, bf16[768,1024]{1,0:T(8,128)(2,1)}, f32[16,8,1024]{2,1,0:T(8,128)}, bf16[256,1024]{1,0:T(8,128)(2,1)}) custom-call(s32[1]{0:T(128)S(6)} %copy.15.counts_ref, bf16[1024,256]{1,0:T(8,128)(2,1)} %feats_hbm.1, f32[1,256]{1,0:T(1,128)} %bitcast.3, bf16[256,768]{1,0:T(8,128)(2,1)} %w_qkv_hbm.1), custom_call_target="tpu_custom_call" | custom-call | tf_op jit(solution)/shard_map/forward/pallas_call | solution.py:150
  34.4 68.5 %backward.1 = (bf16[1024,256]{1,0:T(8,128)(2,1)}, bf16[1024,256]{1,0:T(8,128)(2,1)}, bf16[2,16,16,736]{3,2,1,0:T(8,128)(2,1)}, bf16[2,16,16,240]{3,2,1,0:T(8,128)(2,1)}, bf16[16,16,96]{2,1,0:T(8,128)(2,1)}) custom-call(s32[1]{0:T(128)S(6)} %copy.15.counts_ref, s32[1,1024]{1,0:T(1,128)} %bitcast.5, f32[1,256]{1,0:T(1,128)} %bitcast.4, ...), custom_call_target="tpu_custom_call" | custom-call | tf_op jit(solution)/shard_map/backward/pallas_call | solution.py:664
  102.9 2.9 %finish.1 = (bf16[1024,256]{1,0:T(8,128)(2,1)}, bf16[1024,256]{1,0:T(8,128)(2,1)}, f32[256,768]{1,0:T(8,128)}, f32[256,256]{1,0:T(8,128)}, f32[256,512]{1,0:T(8,128)}, /*index=5*/f32[16,2,16,256]{3,2,1,0:T(8,128)}) custom-call(bf16[1024,256]{1,0:T(8,128)(2,1)} %get-tuple-element.25.result_hbm, bf16[1024,256]{1,0:T(8,128)(2,1)} %get-tuple-element.26.d_feats_hbm, ...), custom_call_target="tpu_custom_call" | custom-call | tf_op jit(solution)/shard_map/finish/pallas_call | solution.py:790

commit v6 on v5

--- a/solution.py
+++ b/solution.py
@@ -742,8 +742,11 @@
             ((qkv_s, qkv_out), (out_s, out_out), (down_s, down_out), (up_s, up_out))
         )
     ]
-    for load in loads:
+    for load in loads[3:] + loads[:3]:
         load.start()
+    for load, one in zip(loads[3:], passes):
+        load.wait()
+        one.start()
     loads[0].wait()
     for core in range(2):
         up_s[:, core] = early_ref[core, :, :, :C1].astype(F32)
@@ -755,10 +758,8 @@
         )
     for store in stores[1:]:
         store.start()
-    for load in loads[1:]:
+    for load in loads[1:3]:
         load.wait()
-    for one in passes:
-        one.start()
     early, late = [
         jnp.concatenate(
             [ref[core, :, :, first:].astype(F32).reshape(C1, -1) for core in range(2)], axis=1

time: 106 us -> 106 us (level)
  no operation moved by 1% of the time
where the time goes in v6:
time: 106 us
  Pallas kernels  104 us (98%)
  between operations  1.45 us (1%)
    pallas_call x1, Pallas kernels, backward_call(): pl.pallas_call(backward_kernel, grid=(STEPS,), in_specs=[pl.BlockSpec(mem...  68.5 us
    pallas_call x1, Pallas kernels, forward_call(): pl.pallas_call(forward_kernel, grid=(STEPS,), in_specs=[pl.BlockSpec(memo...  33.1 us
    pallas_call x1, Pallas kernels, finish_call(): pl.pallas_call(finish_kernel, in_specs=[anywhere] * 5, out_specs=[anywher...  2.88 us

profile of v6, /device:TPU:1, one launch (start us, length us, event | category | flops | bytes accessed | tf_op | source)
XLA Modules:
  0.0 105.9 jit_solution(7102306883422075371)
XLA Ops:
  1.3 33.1 %forward.1 = (bf16[16,1024,1024]{2,1,0:T(8,128)(2,1)}, bf16[768,1024]{1,0:T(8,128)(2,1)}, f32[16,8,1024]{2,1,0:T(8,128)}, bf16[256,1024]{1,0:T(8,128)(2,1)}) custom-call(s32[1]{0:T(128)S(6)} %copy.15.counts_ref, bf16[1024,256]{1,0:T(8,128)(2,1)} %feats_hbm.1, f32[1,256]{1,0:T(1,128)} %bitcast.3, bf16[256,768]{1,0:T(8,128)(2,1)} %w_qkv_hbm.1), custom_call_target="tpu_custom_call" | custom-call | tf_op jit(solution)/shard_map/forward/pallas_call | solution.py:150
  34.4 68.5 %backward.1 = (bf16[1024,256]{1,0:T(8,128)(2,1)}, bf16[1024,256]{1,0:T(8,128)(2,1)}, bf16[2,16,16,736]{3,2,1,0:T(8,128)(2,1)}, bf16[2,16,16,240]{3,2,1,0:T(8,128)(2,1)}, bf16[16,16,96]{2,1,0:T(8,128)(2,1)}) custom-call(s32[1]{0:T(128)S(6)} %copy.15.counts_ref, s32[1,1024]{1,0:T(1,128)} %bitcast.5, f32[1,256]{1,0:T(1,128)} %bitcast.4, ...), custom_call_target="tpu_custom_call" | custom-call | tf_op jit(solution)/shard_map/backward/pallas_call | solution.py:664
  102.9 2.9 %finish.1 = (bf16[1024,256]{1,0:T(8,128)(2,1)}, bf16[1024,256]{1,0:T(8,128)(2,1)}, f32[256,768]{1,0:T(8,128)}, f32[256,256]{1,0:T(8,128)}, f32[256,512]{1,0:T(8,128)}, /*index=5*/f32[16,2,16,256]{3,2,1,0:T(8,128)}) custom-call(bf16[1024,256]{1,0:T(8,128)(2,1)} %get-tuple-element.25.result_hbm, bf16[1024,256]{1,0:T(8,128)(2,1)} %get-tuple-element.26.d_feats_hbm, ...), custom_call_target="tpu_custom_call" | custom-call | tf_op jit(solution)/shard_map/finish/pallas_call | solution.py:791
